TPU v7x, 256 devices: a whole 4x4x8 slice. The times are simulated.
256 devices in a mesh: row: 16 (over x, z_lo, core), col: 16 (over z_hi, y).
Axes of the slice: x: 4, y: 4, z: 8 (z_hi: 4, z_lo: 2; z = z_hi * 2 + z_lo), core: 2. Of those that a mesh axis runs over, the one named last changes fastest.
Arguments:
- pre_act: bfloat16 [2048, 24576], P('row', 'col'), may hold values from -6 to 6
- out_grad: bfloat16 [2048, 12288], P('col', 'row'), may hold values from -4 to 4
- down_weight: bfloat16 [24576, 12288], P('col', 'row'), may hold values from -0.0546875 to 0.0546875
Outputs:
- pre_grad: bfloat16 [2048, 24576], P('row', 'col')
- weight_grad: float32 [24576, 12288], P('col', 'row')
All inputs are finite; a program needn't handle non-finite values.
Results may differ from a plain program's by a relative error of at most 0.0031.
Values may be sent and summed in bfloat16 or wider, within the bound.
No kernel may reach another device: no remote copies, remote signals or barrier semaphores. Data moves between devices by JAX's collectives and lax.ppermute only.
A program may use at most 128 MiB of HBM per device.

v0:
```python
import jax
import jax.numpy as jnp
from jax import lax
from jax.sharding import PartitionSpec as P

coeff_k = 0.7978845608
coeff_c = 0.044715


def gelu_value(z):
    t = jnp.tanh(coeff_k * (z + coeff_c * z * z * z))
    return 0.5 * z * (1.0 + t)


def gelu_slope(z):
    t = jnp.tanh(coeff_k * (z + coeff_c * z * z * z))
    return 0.5 * (1.0 + t) + 0.5 * z * (1.0 - t * t) * coeff_k * (1.0 + 3.0 * coeff_c * z * z)


def contract_rows(left, right):
    return lax.dot_general(
        left, right, (((0,), (0,)), ((), ())), preferred_element_type=jnp.float32
    )


def shards(pre_act, out_grad, down_weight):
    grad_full = lax.all_gather(out_grad, "col", axis=0, tiled=True)
    term = lax.dot_general(
        grad_full, down_weight, (((1,), (1,)), ((), ())), preferred_element_type=jnp.float32
    )
    hidden_grad = lax.psum_scatter(term, "row", scatter_dimension=0, tiled=True)
    pre_float = pre_act.astype(jnp.float32)
    pre_grad = (hidden_grad * gelu_slope(pre_float)).astype(jnp.bfloat16)
    act_piece = gelu_value(
        lax.all_gather(pre_act, "row", axis=0, tiled=True).astype(jnp.float32)
    ).astype(jnp.bfloat16)
    weight_grad = contract_rows(act_piece, grad_full)
    return (pre_grad, weight_grad)


def solution(mesh):
    return jax.shard_map(
        shards,
        mesh=mesh,
        in_specs=(P("row", "col"), P("col", "row"), P("col", "row")),
        out_specs=(P("row", "col"), P("col", "row")),
        check_vma=False,
    )
```

profile of v0, /device:TPU:1, one launch (start us, length us, event | category | flops | bytes accessed | tf_op | source)
XLA Modules:
  0.0 280.2 jit_solution(848659686490421346)
XLA Ops:
  7.2 0.0 copy-start
  7.2 0.0 all-gather.3.cloned.1.call-start
  7.2 0.7 all-gather.3.cloned.1.call-update
  7.9 0.0 all-gather.5.cloned.1.call-start
  8.0 0.7 all-gather.5.cloned.1.call-update
  8.7 0.0 reduce-scatter.2.cloned.1.call-start
  8.7 73.2 %all-gather.3.cloned.1.call-done = bf16[2048,768]{1,0:T(8,128)(2,1)} async-done(((bf16[128,768]{1,0:T(8,128)(2,1)}), bf16[2048,768]{1,0:T(8,128)(2,1)}) %all-gather.3.cloned.1.call-update) | async-done | bytes 3145744 | tf_op jit(solution)/shard_map/all_gather | solution.py:27
  81.9 0.0 copy-done
  81.9 9.9 %fusion.20 = f32[2048,1536]{1,0:T(8,128)} fusion(bf16[2048,768]{1,0:T(8,128)(2,1)} %all-gather.3.cloned.1.call-done, bf16[1536,768]{1,0:T(8,128)(2,1)S(1)} %copy-done), kind=kOutput, calls=%fused_computation.31 | convolution fusion | flops 4831838208 | bytes 18087936 | tf_op jit(solution)/shard_map/dot_general | solution.py:28
  91.8 0.0 reduce-scatter.2.cloned.1.call-update
  91.9 0.0 copy-start.1
  91.9 35.3 %all-gather.5.cloned.1.call-done = bf16[2048,1536]{1,0:T(8,128)(2,1)} async-done(((bf16[128,1536]{1,0:T(8,128)(2,1)}), bf16[2048,1536]{1,0:T(8,128)(2,1)}) %all-gather.5.cloned.1.call-update) | async-done | bytes 6291472 | tf_op jit(solution)/shard_map/all_gather | solution.py:35
  127.2 11.4 %fusion.5 = f32[1536,768]{1,0:T(8,128)} fusion(bf16[2048,768]{1,0:T(8,128)(2,1)} %all-gather.3.cloned.1.call-done, bf16[2048,1536]{1,0:T(8,128)(2,1)} %all-gather.5.cloned.1.call-done), kind=kOutput, calls=%fused_computation.10 | convolution fusion | flops 4863295488 | bytes 14155776 | tf_op jit(solution)/shard_map/dot_general | solution.py:21
  138.6 132.6 %reduce-scatter.2.cloned.1.call-done = f32[128,1536]{1,0:T(8,128)} async-done(((f32[2048,1536]{1,0:T(8,128)}), f32[128,1536]{1,0:T(8,128)}) %reduce-scatter.2.cloned.1.call-update) | async-done | bytes 786448 | tf_op jit(solution)/shard_map/reduce_scatter | solution.py:31
  271.2 0.0 copy-done.1
  271.2 2.4 fusion.14
Async XLA Ops:
  7.2 74.7 %copy-start = (bf16[1536,768]{1,0:T(8,128)(2,1)S(1)}, bf16[1536,768]{1,0:T(8,128)(2,1)}, u32[]{:S(2)}) copy-start(bf16[1536,768]{1,0:T(8,128)(2,1)} %param.5) | copy-start | bytes 7077892
  7.2 74.7 %all-gather.3.cloned.1.call-start = ((), (), s32[]{:S(2)}) async-start(), calls=%async_computation.1 | async-start | bytes 3342336 | tf_op jit(solution)/shard_map/all_gather | solution.py:27
  7.9 119.3 %all-gather.5.cloned.1.call-start = ((), (), s32[]{:S(2)}) async-start(), calls=%async_computation.3 | async-start | bytes 6684672 | tf_op jit(solution)/shard_map/all_gather | solution.py:35
  8.7 262.6 %reduce-scatter.2.cloned.1.call-start = ((), (), s32[]{:S(2)}) async-start(), calls=%async_computation.2 | async-start | bytes 13369344 | tf_op jit(solution)/shard_map/reduce_scatter | solution.py:31
  91.9 179.4 %copy-start.1 = (bf16[128,1536]{1,0:T(8,128)(2,1)S(1)}, bf16[128,1536]{1,0:T(8,128)(2,1)}, u32[]{:S(2)}) copy-start(bf16[128,1536]{1,0:T(8,128)(2,1)} %param.3) | copy-start | bytes 1179652
Sparse Core Ops, SparseCore 0:
  10.4 71.4 all-gather.2
  83.7 43.4 all-gather.4
  129.8 141.3 reduce-scatter.1
where the time goes:
time: 281 us; the launch traced here: 280 us
  waiting for transfers between devices  243 us (86%)
  matrix products  21.3 us (8%)
  between operations  13.8 us (5%)
    reduce_scatter x1, waiting for transfers between devices, shards(): hidden_grad = lax.psum_scatter(term, 'row', scatter_dimension=0, tiled=True)  133 us
    all_gather x1, waiting for transfers between devices, shards(): grad_full = lax.all_gather(out_grad, 'col', axis=0, tiled=True)  73.2 us
    all_gather x1, waiting for transfers between devices, shards(): lax.all_gather(pre_act, 'row', axis=0, tiled=True).astype(jnp.float32)  35.3 us
    dot_general x1, matrix products, contract_rows(): lax.dot_general(left, right, (((0,), (0,)), ((), ())), preferred_element_...  11.4 us
    dot_general x1, matrix products, shards(): lax.dot_general(grad_full, down_weight, (((1,), (1,)), ((), ())), preferr...  9.95 us
  transfers between devices with their start and end apart: 3, of which 3 were waited for; matrix products, arithmetic and copies ran while one was open for 8% of the time, Pallas kernels for 0%

commit v1 on v0

v1 whole, which is shorter than its diff:
```python
import jax
import jax.numpy as jnp
import numpy as np
from jax import lax
from jax.experimental import pallas as pl
from jax.experimental.pallas import tpu as pltpu
from jax.sharding import Mesh, PartitionSpec as P

coeff_k = 0.7978845608
coeff_c = 0.044715

AXES = ("x", "zl", "core", "zh", "y")
SIZES = {"x": 4, "zl": 2, "core": 2, "zh": 4, "y": 4}
TB = 128
MIB = 1024 * 1024
STEPS = ((2, 1), (1, 0), (3, 0), (1, 1), (3, 1), (0, 1), (2, 0), (0, 0))
KEPT = ((0, 0), (2, 0))
WHOLE = pl.BlockSpec(memory_space=pltpu.VMEM)


def fetch(value, axis, ahead):
    n = SIZES[axis]
    return lax.ppermute(value, axis, [((i + ahead) % n, i) for i in range(n)])


def gather_x(copies):
    return lax.all_to_all(copies, "x", 0, 0).reshape(4 * TB, copies.shape[-1])


def send_xz(value, dx, dz):
    pairs = []
    for x in range(4):
        for z in range(2):
            pairs.append((x * 2 + z, (x + dx) % 4 * 2 + (z + dz) % 2))
    return lax.ppermute(value, ("x", "zl"), pairs)


def tanh_of(z):
    return jnp.tanh(coeff_k * (z + coeff_c * z * z * z))


def gelu_kernel(pre_ref, act_ref):
    z = pre_ref[...].astype(jnp.float32)
    act = (0.5 * z * (1.0 + tanh_of(z))).astype(act_ref.dtype)
    for n in range(act_ref.shape[0]):
        act_ref[n] = act


def slope_kernel(pre_ref, slope_ref):
    z = pre_ref[...].astype(jnp.float32)
    t = tanh_of(z)
    slope_ref[...] = 0.5 * (1.0 + t) + 0.5 * z * (1.0 - t * t) * coeff_k * (1.0 + 3.0 * coeff_c * z * z)


def elementwise(kernel, pre_act, dtype, name, copies=None):
    rows, f = pre_act.shape
    tile = 64
    spec = pl.BlockSpec((tile, f), lambda i: (i, 0))
    many = pl.BlockSpec((copies, tile, f), lambda i: (0, i, 0))
    return pl.pallas_call(
        kernel,
        out_shape=jax.ShapeDtypeStruct((copies, rows, f) if copies else (rows, f), dtype),
        grid=(rows // tile,),
        in_specs=[spec],
        out_specs=many if copies else spec,
        compiler_params=pltpu.CompilerParams(vmem_limit_bytes=8 * MIB),
        name=name,
    )(pre_act)


def order_kernel(idx_ref, *refs):
    sources, (own_ref, other_ref) = refs[:-2], refs[-2:]
    n = 0
    for source in sources:
        for b in range(source.shape[0] // TB):
            place = idx_ref[n]
            rows = pl.ds(pl.multiple_of(place % 8 * TB, TB), TB)

            @pl.when(place < 8)
            def _(source=source, b=b, rows=rows):
                own_ref[rows, :] = source[b * TB : (b + 1) * TB, :]

            @pl.when(place >= 8)
            def _(source=source, b=b, rows=rows):
                other_ref[rows, :] = source[b * TB : (b + 1) * TB, :]

            n += 1


def order(index, sources):
    width = sources[0].shape[1]
    out = jax.ShapeDtypeStruct((8 * TB, width), sources[0].dtype)
    return pl.pallas_call(
        order_kernel,
        out_shape=(out, out),
        in_specs=[pl.BlockSpec(memory_space=pltpu.SMEM)] + [WHOLE] * len(sources),
        out_specs=(WHOLE, WHOLE),
        compiler_params=pltpu.CompilerParams(vmem_limit_bytes=16 * MIB),
        name="order_tokens",
    )(index, *sources)


def terms_kernel(own_ref, other_ref, w_own_ref, w_other_ref, *out_refs):
    dims = (((1,), (1,)), ((), ()))
    for n in range(0, len(out_refs), 2):
        rows = slice(n * TB, (n + 2) * TB)
        acc = lax.dot_general(own_ref[rows, :], w_own_ref[...], dims, preferred_element_type=jnp.float32)
        acc += lax.dot_general(other_ref[rows, :], w_other_ref[...], dims, preferred_element_type=jnp.float32)
        out_refs[n][...] = acc[:TB].astype(out_refs[n].dtype)
        out_refs[n + 1][...] = acc[TB:].astype(out_refs[n + 1].dtype)


def terms(own, other, w_own, w_other):
    f, d = w_own.shape
    rows = own.shape[0]
    tile = 512
    grad_spec = pl.BlockSpec((rows, d), lambda i: (0, 0))
    w_spec = pl.BlockSpec((tile, d), lambda i: (i, 0))
    return pl.pallas_call(
        terms_kernel,
        out_shape=[jax.ShapeDtypeStruct((TB, f), jnp.float32 if k in KEPT else jnp.bfloat16) for k in STEPS],
        grid=(f // tile,),
        in_specs=[grad_spec, grad_spec, w_spec, w_spec],
        out_specs=[pl.BlockSpec((TB, tile), lambda i: (0, i))] * len(STEPS),
        compiler_params=pltpu.CompilerParams(vmem_limit_bytes=24 * MIB),
        cost_estimate=pl.CostEstimate(
            flops=4 * rows * f * d, bytes_accessed=4 * (f + rows) * d + 2 * rows * f, transcendentals=0
        ),
        name="terms",
    )(own, other, w_own, w_other)


def weight_kernel(idx_ref, act0_ref, act1_ref, act2_ref, act3_ref, own_ref, other_ref, out_ref, token_ref, grad_ref):
    @pl.when(pl.program_id(0) == 0)
    def _():
        for n in range(16):
            source = own_ref if n < 8 else other_ref
            rows = pl.ds(pl.multiple_of(idx_ref[n] * TB, TB), TB)
            grad_ref[rows, :] = source[n % 8 * TB : (n % 8 + 1) * TB, :]

    dims = (((0,), (0,)), ((), ()))
    quarter = act0_ref.shape[0]
    acc = None
    for n, act_ref in enumerate((act0_ref, act1_ref, act2_ref, act3_ref)):
        rows = slice(n * quarter, (n + 1) * quarter)
        term = lax.dot_general(act_ref[...], grad_ref[rows, :], dims, preferred_element_type=jnp.float32)
        acc = term if acc is None else acc + term
    out_ref[...] = acc
    token_ref[...] = jnp.zeros_like(token_ref)


def weight_product(index, acts, own, other):
    quarter, f = acts[0].shape
    d = own.shape[1]
    tile = 256
    act_spec = pl.BlockSpec((quarter, tile), lambda i: (0, i))
    return pl.pallas_call(
        weight_kernel,
        out_shape=(jax.ShapeDtypeStruct((f, d), jnp.float32), jax.ShapeDtypeStruct((8, 128), jnp.float32)),
        grid=(f // tile,),
        in_specs=[pl.BlockSpec(memory_space=pltpu.SMEM)] + [act_spec] * 4 + [WHOLE, WHOLE],
        out_specs=(pl.BlockSpec((tile, d), lambda i: (i, 0)), pl.BlockSpec((8, 128), lambda i: (0, 0))),
        scratch_shapes=[pltpu.VMEM((4 * quarter, d), own.dtype)],
        compiler_params=pltpu.CompilerParams(vmem_limit_bytes=24 * MIB),
        cost_estimate=pl.CostEstimate(
            flops=8 * quarter * f * d, bytes_accessed=8 * quarter * f + 4 * f * d, transcendentals=0
        ),
        name="weight_grad",
    )(index, *acts, own, other)


def finish_kernel(slope_ref, own_ref, *refs):
    out_ref = refs[-1]
    total = own_ref[...]
    for ref in refs[:-2]:
        total = total + ref[...].astype(jnp.float32)
    out_ref[...] = (total * slope_ref[...]).astype(out_ref.dtype)


def finish(slope, own, received, after):
    rows, f = slope.shape
    return pl.pallas_call(
        finish_kernel,
        out_shape=jax.ShapeDtypeStruct((rows, f), jnp.bfloat16),
        in_specs=[WHOLE] * (2 + len(received)) + [pl.BlockSpec(memory_space=pl.ANY)],
        out_specs=WHOLE,
        compiler_params=pltpu.CompilerParams(vmem_limit_bytes=8 * MIB),
        name="pre_grad",
    )(slope, own, *received, after)


def token_places():
    sizes = [SIZES[a] for a in AXES]
    places, tokens = np.zeros(sizes + [16], np.int32), np.zeros(sizes + [16], np.int32)
    for x, zl, core, zh, y in np.ndindex(*sizes):
        arrival = [(d, e) for d in range(4) for e in range(4)]
        for n, (d, e) in enumerate(arrival):
            yy, zz = (y + d) % 4, (zh + e) % 4
            place = (yy + core) % 2 * 8 + STEPS.index(((zz - x) % 4, (yy // 2 + zl) % 2))
            places[x, zl, core, zh, y, n] = place
            tokens[x, zl, core, zh, y, place] = (yy + core) % 2 * 8 + (yy // 2 + zl) % 2 * 4 + zz
    return np.concatenate([places.reshape(-1, 16), tokens.reshape(-1, 16)], axis=1)


def shards(pre_act, out_grad, down_weight):
    f, d_model = down_weight.shape
    tables = jnp.asarray(token_places())[lax.axis_index(AXES)]

    act = elementwise(gelu_kernel, pre_act, jnp.bfloat16, "gelu", 4)

    along_z = {e: fetch(out_grad, "zh", e) for e in (2, 1, 3)}
    act_x = gather_x(act)
    along_z, act_x = lax.optimization_barrier((along_z, act_x))
    along_z = jnp.concatenate([out_grad, along_z[1], along_z[2], along_z[3]], axis=0)
    far = {d: fetch(along_z, "y", d) for d in (2, 1, 3)}
    act_z = fetch(act_x, "zl", 1)
    act_x_other = fetch(act_x, "core", 1)

    down_weight, act_x_other = lax.optimization_barrier((down_weight, act_x_other))
    w_other = fetch(down_weight, "core", 1)
    grad_own, grad_other = order(tables[:16], [along_z, far[1], far[2], far[3]])
    grad_swapped = fetch(grad_other, "core", 1)
    act_z_other = fetch(act_z, "core", 1)

    part = terms(grad_own, grad_swapped, down_weight, w_other)
    part, act_z_other = lax.optimization_barrier((part, act_z_other))
    part = dict(zip(STEPS, part))
    beside = send_xz(part[2, 1], 0, 1)
    received = [send_xz(part[k], *k) for k in ((1, 0), (3, 0), (1, 1), (3, 1))]
    both = (part[2, 0] + beside.astype(jnp.float32)).astype(jnp.bfloat16)
    received.append(send_xz(both, 2, 0))
    part[0, 1], both = lax.optimization_barrier((part[0, 1], both))
    received.append(send_xz(part[0, 1], 0, 1))

    slope = elementwise(slope_kernel, pre_act, jnp.float32, "slope")
    tables, slope, both = lax.optimization_barrier((tables, slope, both))
    weight_grad, done = weight_product(tables[16:], (act_x, act_z, act_x_other, act_z_other), grad_own, grad_other)
    pre_grad = finish(slope, part[0, 0], received, done)
    return (pre_grad, weight_grad)


def solution(mesh):
    fine = Mesh(mesh.devices.reshape(tuple(SIZES[a] for a in AXES)), AXES)
    row, col = ("x", "zl", "core"), ("zh", "y")
    return jax.shard_map(
        shards,
        mesh=fine,
        in_specs=(P(row, col), P(col, row), P(col, row)),
        out_specs=(P(row, col), P(col, row)),
        check_vma=False,
    )
```

time: 281 us -> 128 us (0.46)
  waiting for transfers between devices: 243 us -> 61.4 us
  starting transfers between devices: 0.11 us -> 41.8 us
  matrix products: 21.3 us -> 0 us
  Pallas kernels: 0 us -> 20.4 us
  between operations: 13.8 us -> 0.73 us
  local copies, waits for them, and re-layouts: 0.02 us -> 2.98 us
    reduce_scatter x1 -> x0, waiting for transfers between devices: 133 us -> none  [shards(): hidden_grad = lax.psum_scatter(term, 'row', scatter_dimension=0, tiled=True)]
    all_gather x2 -> x0, waiting for transfers between devices: 109 us -> none  [the longest x1 73.2 us: shards(): grad_full = lax.all_gather(out_grad, 'col', axis=0, tiled=True)]
    ppermute x0 -> x18, waiting for transfers between devices: none -> 61.4 us  [the longest x11 49.5 us: fetch(): return lax.ppermute(value, axis, [((i + ahead) % n, i) for i in range(n)])]
    ppermute x0 -> x18, starting transfers between devices: none -> 36.8 us  [the longest x11 21.1 us: fetch(): return lax.ppermute(value, axis, [((i + ahead) % n, i) for i in range(n)])]
    dot_general x2 -> x0, matrix products: 21.3 us -> none  [the longest x1 11.4 us: contract_rows(): lax.dot_general(left, right, (((0,), (0,)), ((), ())), preferred_element_...]
    pallas_call x0 -> x6, Pallas kernels: none -> 20.4 us  [the longest x1 8.64 us: weight_product(): pl.pallas_call(weight_kernel, out_shape=(jax.ShapeDtypeStruct((f, d), jnp...]
    all_to_all x0 -> x1, starting transfers between devices: none -> 4.97 us  [gather_x(): return lax.all_to_all(copies, 'x', 0, 0).reshape(4 * TB, copies.shape[-1])]
  transfers between devices with their start and end apart: 3 -> 19, of which waited for: 3 -> 10; matrix products, arithmetic and copies ran while one was open for 8% -> 1% of each run, Pallas kernels for 0% -> 14%
where the time goes in v1:
time: 128 us; the launch traced here: 127 us
  waiting for transfers between devices  61.4 us (48%)
  starting transfers between devices  41.8 us (33%)
  Pallas kernels  20.4 us (16%)
  local copies, waits for them, and re-layouts  2.98 us (2%)
    ppermute x11, waiting for transfers between devices, fetch(): return lax.ppermute(value, axis, [((i + ahead) % n, i) for i in range(n)])  49.5 us
    ppermute x11, starting transfers between devices, fetch(): return lax.ppermute(value, axis, [((i + ahead) % n, i) for i in range(n)])  21.1 us
    ppermute x7, starting transfers between devices, send_xz(): return lax.ppermute(value, ('x', 'zl'), pairs)  15.7 us
    ppermute x7, waiting for transfers between devices, send_xz(): return lax.ppermute(value, ('x', 'zl'), pairs)  11.9 us
    pallas_call x1, Pallas kernels, weight_product(): pl.pallas_call(weight_kernel, out_shape=(jax.ShapeDtypeStruct((f, d), jnp...  8.64 us
    pallas_call x1, Pallas kernels, terms(): pl.pallas_call(terms_kernel, out_shape=[jax.ShapeDtypeStruct((TB, f), jnp...  6.95 us
    all_to_all x1, starting transfers between devices, gather_x(): return lax.all_to_all(copies, 'x', 0, 0).reshape(4 * TB, copies.shape[-1])  4.97 us
  transfers between devices with their start and end apart: 19, of which 10 were waited for; matrix products, arithmetic and copies ran while one was open for 1% of the time, Pallas kernels for 14%

profile of v1, /device:TPU:1, one launch (start us, length us, event | category | flops | bytes accessed | tf_op | source)
XLA Modules:
  0.0 127.3 jit_solution(14022869896441788894)
XLA Ops:
  0.6 0.0 copy-start
  0.6 1.0 copy-done
  1.6 1.3 %gelu.1 = bf16[4,128,1536]{2,1,0:T(8,128)(2,1)} custom-call(bf16[128,1536]{1,0:T(8,128)(2,1)S(1)} %copy-done), custom_call_target="tpu_custom_call" | custom-call | tf_op jit(solution)/shard_map/gelu/pallas_call | solution.py:60
  2.9 0.0 copy-start.5
  2.9 5.0 %all-to-all-start = ((bf16[4,128,1536]{2,1,0:T(8,128)(2,1)}), bf16[4,128,1536]{2,1,0:T(8,128)(2,1)S(1)}, u32[]{:S(2)}, u32[]{:S(2)}) async-start(bf16[4,128,1536]{2,1,0:T(8,128)(2,1)} %gelu.1), calls=%async_computation | async-start | bytes 3145728 | tf_op jit(solution)/shard_map/all_to_all | solution.py:27
  7.9 0.0 copy-done.5
  7.9 6.0 %collective-permute-start = (bf16[128,768]{1,0:T(8,128)(2,1)S(1)}, bf16[128,768]{1,0:T(8,128)(2,1)S(1)}, u32[]{:S(2)}, u32[]{:S(2)}) collective-permute-start(bf16[128,768]{1,0:T(8,128)(2,1)S(1)} %copy-done.5), channel_id=1, source_target_pairs={{4,0},{8,4},{12,8},{0,12},{5,1},{9,5},{13,9},{1,13},{6,2},{10,6},{... | collective-permute-start | bytes 589832 | tf_op jit(solution)/shard_map/ppermute | solution.py:23
  13.9 1.0 collective-permute-start.1
  14.9 2.3 %collective-permute-start.2 = (bf16[128,768]{1,0:T(8,128)(2,1)S(1)}, bf16[128,768]{1,0:T(8,128)(2,1)S(1)}, u32[]{:S(2)}, u32[]{:S(2)}) collective-permute-start(bf16[128,768]{1,0:T(8,128)(2,1)S(1)} %copy-done.5), channel_id=1, source_target_pairs={{12,0},{0,4},{4,8},{8,12},{13,1},{1,5},{5,9},{9,13},{14,2},{2,6},{... | collective-permute-start | bytes 589832 | tf_op jit(solution)/shard_map/ppermute | solution.py:23
  17.2 3.8 %collective-permute-done = bf16[128,768]{1,0:T(8,128)(2,1)S(1)} collective-permute-done((bf16[128,768]{1,0:T(8,128)(2,1)S(1)}, bf16[128,768]{1,0:T(8,128)(2,1)S(1)}, u32[]{:S(2)}, u32[]{:S(2)}) %collective-permute-start) | collective-permute-done | bytes 196640 | tf_op jit(solution)/shard_map/ppermute | solution.py:23
  20.9 6.4 %collective-permute-done.1 = bf16[128,768]{1,0:T(8,128)(2,1)S(1)} collective-permute-done((bf16[128,768]{1,0:T(8,128)(2,1)S(1)}, bf16[128,768]{1,0:T(8,128)(2,1)S(1)}, u32[]{:S(2)}, u32[]{:S(2)}) %collective-permute-start.1) | collective-permute-done | bytes 196640 | tf_op jit(solution)/shard_map/ppermute | solution.py:23
  27.3 1.3 %collective-permute-done.2 = bf16[128,768]{1,0:T(8,128)(2,1)S(1)} collective-permute-done((bf16[128,768]{1,0:T(8,128)(2,1)S(1)}, bf16[128,768]{1,0:T(8,128)(2,1)S(1)}, u32[]{:S(2)}, u32[]{:S(2)}) %collective-permute-start.2) | collective-permute-done | bytes 196640 | tf_op jit(solution)/shard_map/ppermute | solution.py:23
  28.7 0.0 all-to-all-done
  28.7 3.1 %collective-permute-start.7 = (bf16[512,1536]{1,0:T(8,128)(2,1)S(1)}, bf16[512,1536]{1,0:T(8,128)(2,1)S(1)}, u32[]{:S(2)}, u32[]{:S(2)}) collective-permute-start(bf16[512,1536]{1,0:T(8,128)(2,1)S(1)} %bitcast.5), channel_id=1, source_target_pairs={{16,0},{0,16},{17,1},{1,17},{18,2},{2,18},{19,3},{3,19},{20,4},{4,... | collective-permute-start | bytes 4718600 | tf_op jit(solution)/shard_map/ppermute | solution.py:23
  31.8 3.1 %collective-permute-start.9 = (bf16[512,1536]{1,0:T(8,128)(2,1)S(1)}, bf16[512,1536]{1,0:T(8,128)(2,1)}, u32[]{:S(2)}, u32[]{:S(2)}) collective-permute-start(bf16[512,1536]{1,0:T(8,128)(2,1)S(1)} %bitcast.6), channel_id=1, source_target_pairs={{32,0},{0,32},{33,1},{1,33},{34,2},{2,34},{35,3},{3,35},{36,4},{4,... | collective-permute-start | bytes 4718600 | tf_op jit(solution)/shard_map/ppermute | solution.py:23
  35.0 2.8 %collective-permute-start.3 = (bf16[512,768]{1,0:T(8,128)(2,1)S(1)}, bf16[512,768]{1,0:T(8,128)(2,1)S(1)}, u32[]{:S(2)}, u32[]{:S(2)}) collective-permute-start(bf16[512,768]{1,0:T(8,128)(2,1)S(1)} %constant_dynamic-update-slice_fusion.refs_0_), channel_id=1, source_target_pairs={{1,0},{2,1},{3,2},{0,3},{5,4},{6,5},{7,6},{4,7},{9,8},{10,9},{11,1... | collective-permute-start | bytes 2359304 | tf_op jit(solution)/shard_map/ppermute | solution.py:23
  37.8 0.3 collective-permute-start.4
  38.1 0.7 collective-permute-start.5
  38.8 0.0 collective-permute-done.7.act2_ref
  38.8 0.0 copy-start.3
  38.8 1.1 copy-done.3
  40.0 1.1 collective-permute-start.8
  41.1 0.7 constant_dynamic-slice_fusion
  41.8 0.0 copy-start.2
  41.8 29.4 %collective-permute-done.3.refs_1_ = bf16[512,768]{1,0:T(8,128)(2,1)S(1)} collective-permute-done((bf16[512,768]{1,0:T(8,128)(2,1)S(1)}, bf16[512,768]{1,0:T(8,128)(2,1)S(1)}, u32[]{:S(2)}, u32[]{:S(2)}) %collective-permute-start.3) | collective-permute-done | bytes 786464 | tf_op jit(solution)/shard_map/ppermute | solution.py:23
  71.1 0.0 collective-permute-done.4.refs_2_
  71.2 4.6 %collective-permute-done.5.refs_3_ = bf16[512,768]{1,0:T(8,128)(2,1)} collective-permute-done((bf16[512,768]{1,0:T(8,128)(2,1)S(1)}, bf16[512,768]{1,0:T(8,128)(2,1)}, u32[]{:S(2)}, u32[]{:S(2)}) %collective-permute-start.5) | collective-permute-done | bytes 786464 | tf_op jit(solution)/shard_map/ppermute | solution.py:23
  75.7 1.8 %order_tokens.1 = (bf16[1024,768]{1,0:T(8,128)(2,1)S(1)}, bf16[1024,768]{1,0:T(8,128)(2,1)S(1)}) custom-call(s32[16]{0:T(128)S(1)} %slice_bitcast_fusion.idx_ref, bf16[512,768]{1,0:T(8,128)(2,1)S(1)} %constant_dynamic-update-slice_fusion.refs_0_, bf16[512,768]{1,0:T(8,128)(2,1)S(1)} %collective-permute-done.3.refs_1_, ...), custom_call_target="tpu_custom_call" | custom-call | tf_op jit(solution)/shard_map/order_tokens/pallas_call | solution.py:93
  77.5 0.6 collective-permute-start.6
  78.1 0.0 collective-permute-done.9.act1_ref
  78.1 0.1 collective-permute-start.10
  78.2 4.1 %collective-permute-done.6.other_ref = bf16[1024,768]{1,0:T(8,128)(2,1)S(1)} collective-permute-done((bf16[1024,768]{1,0:T(8,128)(2,1)S(1)}, bf16[1024,768]{1,0:T(8,128)(2,1)S(1)}, u32[]{:S(2)}, u32[]{:S(2)}) %collective-permute-start.6) | collective-permute-done | bytes 1572896 | tf_op jit(solution)/shard_map/ppermute | solution.py:23
  82.3 0.0 collective-permute-done.8.w_other_ref
  82.3 0.0 copy-done.2
  82.3 0.0 copy-start.1
  82.3 6.9 %terms.1 = (bf16[128,1536]{1,0:T(8,128)(2,1)S(1)}, bf16[128,1536]{1,0:T(8,128)(2,1)S(1)}, bf16[128,1536]{1,0:T(8,128)(2,1)S(1)}, bf16[128,1536]{1,0:T(8,128)(2,1...) custom-call(bf16[1024,768]{1,0:T(8,128)(2,1)S(1)} %get-tuple-element, ...), custom_call_target="tpu_custom_call" | custom-call | flops 4831838208 | bytes 11010048 | tf_op jit(solution)/shard_map/terms/pallas_call | solution.py:119
  89.2 0.0 copy-start.4
  89.2 0.0 collective-permute-done.10.act3_ref
  89.3 0.1 collective-permute-start.15
  89.4 0.0 copy-done.1
  89.4 0.5 slope.1.slope_ref
  89.9 0.1 slice.11.idx_ref
  90.0 1.5 %collective-permute-start.11 = (bf16[128,1536]{1,0:T(8,128)(2,1)S(1)}, bf16[128,1536]{1,0:T(8,128)(2,1)S(1)}, u32[]{:S(2)}, u32[]{:S(2)}) collective-permute-start(bf16[128,1536]{1,0:T(8,128)(2,1)S(1)} %get-tuple-element.49), channel_id=1, source_target_pairs={{0,64},{32,96},{64,128},{96,160},{128,192},{160,224},{192,0},{224,... | collective-permute-start | bytes 1179656 | tf_op jit(solution)/shard_map/ppermute | solution.py:35
  91.5 1.3 %collective-permute-start.12 = (bf16[128,1536]{1,0:T(8,128)(2,1)S(1)}, bf16[128,1536]{1,0:T(8,128)(2,1)S(1)}, u32[]{:S(2)}, u32[]{:S(2)}) collective-permute-start(bf16[128,1536]{1,0:T(8,128)(2,1)S(1)} %get-tuple-element.50), channel_id=1, source_target_pairs={{0,192},{32,224},{64,0},{96,32},{128,64},{160,96},{192,128},{224,1... | collective-permute-start | bytes 1179656 | tf_op jit(solution)/shard_map/ppermute | solution.py:35
  92.8 1.3 %collective-permute-start.13 = (bf16[128,1536]{1,0:T(8,128)(2,1)S(1)}, bf16[128,1536]{1,0:T(8,128)(2,1)S(1)}, u32[]{:S(2)}, u32[]{:S(2)}) collective-permute-start(bf16[128,1536]{1,0:T(8,128)(2,1)S(1)} %get-tuple-element.51), channel_id=1, source_target_pairs={{0,96},{32,64},{64,160},{96,128},{128,224},{160,192},{192,32},{224... | collective-permute-start | bytes 1179656 | tf_op jit(solution)/shard_map/ppermute | solution.py:35
  94.1 2.3 %collective-permute-start.14 = (bf16[128,1536]{1,0:T(8,128)(2,1)S(1)}, bf16[128,1536]{1,0:T(8,128)(2,1)S(1)}, u32[]{:S(2)}, u32[]{:S(2)}) collective-permute-start(bf16[128,1536]{1,0:T(8,128)(2,1)S(1)} %get-tuple-element.52), channel_id=1, source_target_pairs={{0,224},{32,192},{64,32},{96,0},{128,96},{160,64},{192,160},{224,1... | collective-permute-start | bytes 1179656 | tf_op jit(solution)/shard_map/ppermute | solution.py:35
  96.4 3.3 %collective-permute-done.15 = bf16[128,1536]{1,0:T(8,128)(2,1)S(1)} collective-permute-done((bf16[128,1536]{1,0:T(8,128)(2,1)S(1)}, bf16[128,1536]{1,0:T(8,128)(2,1)S(1)}, u32[]{:S(2)}, u32[]{:S(2)}) %collective-permute-start.15) | collective-permute-done | bytes 393248 | tf_op jit(solution)/shard_map/ppermute | solution.py:35
  99.7 0.1 add_convert_fusion
  99.7 3.1 %collective-permute-start.16 = (bf16[128,1536]{1,0:T(8,128)(2,1)S(1)}, bf16[128,1536]{1,0:T(8,128)(2,1)S(1)}, u32[]{:S(2)}, u32[]{:S(2)}) collective-permute-start(bf16[128,1536]{1,0:T(8,128)(2,1)S(1)} %add_convert_fusion), channel_id=1, source_target_pairs={{0,128},{32,160},{64,192},{96,224},{128,0},{160,32},{192,64},{224,... | collective-permute-start | bytes 1179656 | tf_op jit(solution)/shard_map/ppermute | solution.py:35
  102.8 0.0 collective-permute-done.11.refs_0_
  102.8 6.2 %collective-permute-start.17 = (bf16[128,1536]{1,0:T(8,128)(2,1)S(1)}, bf16[128,1536]{1,0:T(8,128)(2,1)S(1)}, u32[]{:S(2)}, u32[]{:S(2)}) collective-permute-start(bf16[128,1536]{1,0:T(8,128)(2,1)S(1)} %get-tuple-element.56), channel_id=1, source_target_pairs={{0,32},{32,0},{64,96},{96,64},{128,160},{160,128},{192,224},{224,1... | collective-permute-start | bytes 1179656 | tf_op jit(solution)/shard_map/ppermute | solution.py:35
  109.0 0.0 copy-done.4
  109.0 8.6 %weight_grad.1 = (f32[1536,768]{1,0:T(8,128)}, f32[8,128]{1,0:T(8,128)S(1)}) custom-call(s32[16]{0:T(128)S(1)} %slice.11.idx_ref, bf16[512,1536]{1,0:T(8,128)(2,1)S(1)} %bitcast.7, bf16[512,1536]{1,0:T(8,128)(2,1)} %collective-permute-done.9.act1_ref, bf16[512,1536]{1,0:T(8,128)(2,1)S(1)} %copy-done.4, ...), custom_call_target="tpu_custom_call" | custom-call | flops 4831838208 | bytes 11010048 | tf_op jit(solution)/shard_map/weight_grad/pallas_call | solution.py:157
  117.6 0.0 collective-permute-done.12.refs_1_
  117.6 0.0 collective-permute-done.13.refs_2_
  117.6 0.2 collective-permute-done.14.refs_3_
  117.8 2.4 %collective-permute-done.16.refs_4_ = bf16[128,1536]{1,0:T(8,128)(2,1)S(1)} collective-permute-done((bf16[128,1536]{1,0:T(8,128)(2,1)S(1)}, bf16[128,1536]{1,0:T(8,128)(2,1)S(1)}, u32[]{:S(2)}, u32[]{:S(2)}) %collective-permute-start.16) | collective-permute-done | bytes 393248 | tf_op jit(solution)/shard_map/ppermute | solution.py:35
  120.1 6.0 %collective-permute-done.17.refs_5_ = bf16[128,1536]{1,0:T(8,128)(2,1)S(1)} collective-permute-done((bf16[128,1536]{1,0:T(8,128)(2,1)S(1)}, bf16[128,1536]{1,0:T(8,128)(2,1)S(1)}, u32[]{:S(2)}, u32[]{:S(2)}) %collective-permute-start.17) | collective-permute-done | bytes 393248 | tf_op jit(solution)/shard_map/ppermute | solution.py:35
  126.2 1.2 pre_grad.1
  (5 shorter events, 0.1 us)
Async XLA Ops:
  0.6 1.0 copy-start
  2.9 5.0 %copy-start.5 = (bf16[128,768]{1,0:T(8,128)(2,1)S(1)}, bf16[128,768]{1,0:T(8,128)(2,1)}, u32[]{:S(2)}) copy-start(bf16[128,768]{1,0:T(8,128)(2,1)} %param.5) | copy-start | bytes 589828
  2.9 25.8 %all-to-all-start = ((bf16[4,128,1536]{2,1,0:T(8,128)(2,1)}), bf16[4,128,1536]{2,1,0:T(8,128)(2,1)S(1)}, u32[]{:S(2)}, u32[]{:S(2)}) async-start(bf16[4,128,1536]{2,1,0:T(8,128)(2,1)} %gelu.1), calls=%async_computation | async-start | bytes 3145728 | tf_op jit(solution)/shard_map/all_to_all | solution.py:27
  7.9 13.1 %collective-permute-start = (bf16[128,768]{1,0:T(8,128)(2,1)S(1)}, bf16[128,768]{1,0:T(8,128)(2,1)S(1)}, u32[]{:S(2)}, u32[]{:S(2)}) collective-permute-start(bf16[128,768]{1,0:T(8,128)(2,1)S(1)} %copy-done.5), channel_id=1, source_target_pairs={{4,0},{8,4},{12,8},{0,12},{5,1},{9,5},{13,9},{1,13},{6,2},{10,6},{... | collective-permute-start | bytes 589832 | tf_op jit(solution)/shard_map/ppermute | solution.py:23
  13.9 13.4 %collective-permute-start.1 = (bf16[128,768]{1,0:T(8,128)(2,1)S(1)}, bf16[128,768]{1,0:T(8,128)(2,1)S(1)}, u32[]{:S(2)}, u32[]{:S(2)}) collective-permute-start(bf16[128,768]{1,0:T(8,128)(2,1)S(1)} %copy-done.5), channel_id=1, source_target_pairs={{8,0},{12,4},{0,8},{4,12},{9,1},{13,5},{1,9},{5,13},{10,2},{14,6},... | collective-permute-start | bytes 589832 | tf_op jit(solution)/shard_map/ppermute | solution.py:23
  14.9 13.8 %collective-permute-start.2 = (bf16[128,768]{1,0:T(8,128)(2,1)S(1)}, bf16[128,768]{1,0:T(8,128)(2,1)S(1)}, u32[]{:S(2)}, u32[]{:S(2)}) collective-permute-start(bf16[128,768]{1,0:T(8,128)(2,1)S(1)} %copy-done.5), channel_id=1, source_target_pairs={{12,0},{0,4},{4,8},{8,12},{13,1},{1,5},{5,9},{9,13},{14,2},{2,6},{... | collective-permute-start | bytes 589832 | tf_op jit(solution)/shard_map/ppermute | solution.py:23
  28.7 10.1 %collective-permute-start.7 = (bf16[512,1536]{1,0:T(8,128)(2,1)S(1)}, bf16[512,1536]{1,0:T(8,128)(2,1)S(1)}, u32[]{:S(2)}, u32[]{:S(2)}) collective-permute-start(bf16[512,1536]{1,0:T(8,128)(2,1)S(1)} %bitcast.5), channel_id=1, source_target_pairs={{16,0},{0,16},{17,1},{1,17},{18,2},{2,18},{19,3},{3,19},{20,4},{4,... | collective-permute-start | bytes 4718600 | tf_op jit(solution)/shard_map/ppermute | solution.py:23
  31.8 46.3 %collective-permute-start.9 = (bf16[512,1536]{1,0:T(8,128)(2,1)S(1)}, bf16[512,1536]{1,0:T(8,128)(2,1)}, u32[]{:S(2)}, u32[]{:S(2)}) collective-permute-start(bf16[512,1536]{1,0:T(8,128)(2,1)S(1)} %bitcast.6), channel_id=1, source_target_pairs={{32,0},{0,32},{33,1},{1,33},{34,2},{2,34},{35,3},{3,35},{36,4},{4,... | collective-permute-start | bytes 4718600 | tf_op jit(solution)/shard_map/ppermute | solution.py:23
  35.0 36.2 %collective-permute-start.3 = (bf16[512,768]{1,0:T(8,128)(2,1)S(1)}, bf16[512,768]{1,0:T(8,128)(2,1)S(1)}, u32[]{:S(2)}, u32[]{:S(2)}) collective-permute-start(bf16[512,768]{1,0:T(8,128)(2,1)S(1)} %constant_dynamic-update-slice_fusion.refs_0_), channel_id=1, source_target_pairs={{1,0},{2,1},{3,2},{0,3},{5,4},{6,5},{7,6},{4,7},{9,8},{10,9},{11,1... | collective-permute-start | bytes 2359304 | tf_op jit(solution)/shard_map/ppermute | solution.py:23
  37.8 33.4 %collective-permute-start.4 = (bf16[512,768]{1,0:T(8,128)(2,1)S(1)}, bf16[512,768]{1,0:T(8,128)(2,1)}, u32[]{:S(2)}, u32[]{:S(2)}) collective-permute-start(bf16[512,768]{1,0:T(8,128)(2,1)S(1)} %constant_dynamic-update-slice_fusion.refs_0_), channel_id=1, source_target_pairs={{2,0},{3,1},{0,2},{1,3},{6,4},{7,5},{4,6},{5,7},{10,8},{11,9},{8,1... | collective-permute-start | bytes 2359304 | tf_op jit(solution)/shard_map/ppermute | solution.py:23
  38.1 37.6 %collective-permute-start.5 = (bf16[512,768]{1,0:T(8,128)(2,1)S(1)}, bf16[512,768]{1,0:T(8,128)(2,1)}, u32[]{:S(2)}, u32[]{:S(2)}) collective-permute-start(bf16[512,768]{1,0:T(8,128)(2,1)S(1)} %constant_dynamic-update-slice_fusion.refs_0_), channel_id=1, source_target_pairs={{3,0},{0,1},{1,2},{2,3},{7,4},{4,5},{5,6},{6,7},{11,8},{8,9},{9,10... | collective-permute-start | bytes 2359304 | tf_op jit(solution)/shard_map/ppermute | solution.py:23
  38.8 1.1 copy-start.3
  40.0 42.3 %collective-permute-start.8 = (bf16[1536,768]{1,0:T(8,128)(2,1)}, bf16[1536,768]{1,0:T(8,128)(2,1)}, u32[]{:S(2)}, u32[]{:S(2)}) collective-permute-start(bf16[1536,768]{1,0:T(8,128)(2,1)} %w_own_ref), channel_id=1, source_target_pairs={{16,0},{0,16},{17,1},{1,17},{18,2},{2,18},{19,3},{3,19},{20,4},{4,... | collective-permute-start | bytes 7077896 | tf_op jit(solution)/shard_map/ppermute | solution.py:23
  41.8 40.5 %copy-start.2 = (bf16[1536,768]{1,0:T(8,128)(2,1)S(1)}, bf16[1536,768]{1,0:T(8,128)(2,1)}, u32[]{:S(2)}) copy-start(bf16[1536,768]{1,0:T(8,128)(2,1)} %w_own_ref) | copy-start | bytes 7077892
  77.5 4.8 %collective-permute-start.6 = (bf16[1024,768]{1,0:T(8,128)(2,1)S(1)}, bf16[1024,768]{1,0:T(8,128)(2,1)S(1)}, u32[]{:S(2)}, u32[]{:S(2)}) collective-permute-start(bf16[1024,768]{1,0:T(8,128)(2,1)S(1)} %get-tuple-element.37.other_ref), channel_id=1, source_target_pairs={{16,0},{0,16},{17,1},{1,17},{18,2},{2,18},{19,3},{3,19},{20,4},{4,... | collective-permute-start | bytes 4718600 | tf_op jit(solution)/shard_map/ppermute | solution.py:23
  78.1 11.2 %collective-permute-start.10 = (bf16[512,1536]{1,0:T(8,128)(2,1)}, bf16[512,1536]{1,0:T(8,128)(2,1)S(1)}, u32[]{:S(2)}, u32[]{:S(2)}) collective-permute-start(bf16[512,1536]{1,0:T(8,128)(2,1)} %collective-permute-done.9.act1_ref), channel_id=1, source_target_pairs={{16,0},{0,16},{17,1},{1,17},{18,2},{2,18},{19,3},{3,19},{20,4},{4,... | collective-permute-start | bytes 4718600 | tf_op jit(solution)/shard_map/ppermute | solution.py:23
  82.3 7.1 %copy-start.1 = (bf16[128,1536]{1,0:T(8,128)(2,1)S(1)}, bf16[128,1536]{1,0:T(8,128)(2,1)}, u32[]{:S(2)}) copy-start(bf16[128,1536]{1,0:T(8,128)(2,1)} %pre_ref.3) | copy-start | bytes 1179652
  89.2 19.7 %copy-start.4 = (bf16[512,1536]{1,0:T(8,128)(2,1)S(1)}, bf16[512,1536]{1,0:T(8,128)(2,1)}, u32[]{:S(2)}) copy-start(bf16[512,1536]{1,0:T(8,128)(2,1)} %copy-done.3) | copy-start | bytes 4718596
  89.3 10.4 %collective-permute-start.15 = (bf16[128,1536]{1,0:T(8,128)(2,1)S(1)}, bf16[128,1536]{1,0:T(8,128)(2,1)S(1)}, u32[]{:S(2)}, u32[]{:S(2)}) collective-permute-start(bf16[128,1536]{1,0:T(8,128)(2,1)S(1)} %get-tuple-element.54), channel_id=1, source_target_pairs={{0,32},{32,0},{64,96},{96,64},{128,160},{160,128},{192,224},{224,1... | collective-permute-start | bytes 1179656 | tf_op jit(solution)/shard_map/ppermute | solution.py:35
  90.0 12.8 %collective-permute-start.11 = (bf16[128,1536]{1,0:T(8,128)(2,1)S(1)}, bf16[128,1536]{1,0:T(8,128)(2,1)S(1)}, u32[]{:S(2)}, u32[]{:S(2)}) collective-permute-start(bf16[128,1536]{1,0:T(8,128)(2,1)S(1)} %get-tuple-element.49), channel_id=1, source_target_pairs={{0,64},{32,96},{64,128},{96,160},{128,192},{160,224},{192,0},{224,... | collective-permute-start | bytes 1179656 | tf_op jit(solution)/shard_map/ppermute | solution.py:35
  91.5 26.1 %collective-permute-start.12 = (bf16[128,1536]{1,0:T(8,128)(2,1)S(1)}, bf16[128,1536]{1,0:T(8,128)(2,1)S(1)}, u32[]{:S(2)}, u32[]{:S(2)}) collective-permute-start(bf16[128,1536]{1,0:T(8,128)(2,1)S(1)} %get-tuple-element.50), channel_id=1, source_target_pairs={{0,192},{32,224},{64,0},{96,32},{128,64},{160,96},{192,128},{224,1... | collective-permute-start | bytes 1179656 | tf_op jit(solution)/shard_map/ppermute | solution.py:35
  92.8 24.8 %collective-permute-start.13 = (bf16[128,1536]{1,0:T(8,128)(2,1)S(1)}, bf16[128,1536]{1,0:T(8,128)(2,1)S(1)}, u32[]{:S(2)}, u32[]{:S(2)}) collective-permute-start(bf16[128,1536]{1,0:T(8,128)(2,1)S(1)} %get-tuple-element.51), channel_id=1, source_target_pairs={{0,96},{32,64},{64,160},{96,128},{128,224},{160,192},{192,32},{224... | collective-permute-start | bytes 1179656 | tf_op jit(solution)/shard_map/ppermute | solution.py:35
  94.1 23.7 %collective-permute-start.14 = (bf16[128,1536]{1,0:T(8,128)(2,1)S(1)}, bf16[128,1536]{1,0:T(8,128)(2,1)S(1)}, u32[]{:S(2)}, u32[]{:S(2)}) collective-permute-start(bf16[128,1536]{1,0:T(8,128)(2,1)S(1)} %get-tuple-element.52), channel_id=1, source_target_pairs={{0,224},{32,192},{64,32},{96,0},{128,96},{160,64},{192,160},{224,1... | collective-permute-start | bytes 1179656 | tf_op jit(solution)/shard_map/ppermute | solution.py:35
  99.7 20.4 %collective-permute-start.16 = (bf16[128,1536]{1,0:T(8,128)(2,1)S(1)}, bf16[128,1536]{1,0:T(8,128)(2,1)S(1)}, u32[]{:S(2)}, u32[]{:S(2)}) collective-permute-start(bf16[128,1536]{1,0:T(8,128)(2,1)S(1)} %add_convert_fusion), channel_id=1, source_target_pairs={{0,128},{32,160},{64,192},{96,224},{128,0},{160,32},{192,64},{224,... | collective-permute-start | bytes 1179656 | tf_op jit(solution)/shard_map/ppermute | solution.py:35
  102.8 23.4 %collective-permute-start.17 = (bf16[128,1536]{1,0:T(8,128)(2,1)S(1)}, bf16[128,1536]{1,0:T(8,128)(2,1)S(1)}, u32[]{:S(2)}, u32[]{:S(2)}) collective-permute-start(bf16[128,1536]{1,0:T(8,128)(2,1)S(1)} %get-tuple-element.56), channel_id=1, source_target_pairs={{0,32},{32,0},{64,96},{96,64},{128,160},{160,128},{192,224},{224,1... | collective-permute-start | bytes 1179656 | tf_op jit(solution)/shard_map/ppermute | solution.py:35

commit v2 on v1

v2 whole, which is shorter than its diff:
```python
import jax
import jax.numpy as jnp
import numpy as np
from jax import lax
from jax.experimental import pallas as pl
from jax.experimental.pallas import tpu as pltpu
from jax.sharding import Mesh, PartitionSpec as P

coeff_k = 0.7978845608
coeff_c = 0.044715

AXES = ("x", "zl", "core", "zh", "y")
SIZES = {"x": 4, "zl": 2, "core": 2, "zh": 4, "y": 4}
TB = 128
MIB = 1024 * 1024
STEPS = ((2, 1), (1, 0), (3, 0), (1, 1), (3, 1), (2, 0), (0, 1), (0, 0))
KEPT = ((0, 0), (2, 0), (0, 1))
WHOLE = pl.BlockSpec(memory_space=pltpu.VMEM)


def in_vmem(value):
    return pltpu.with_memory_space_constraint(value, pltpu.VMEM)


def in_hbm(value):
    return pltpu.with_memory_space_constraint(value, pltpu.HBM)


def fetch(value, axis, ahead):
    n = SIZES[axis]
    return lax.ppermute(value, axis, [((i + ahead) % n, i) for i in range(n)])


def repeat_kernel(*refs):
    sources, (out_ref, sems) = refs[:-2], refs[-2:]
    copies = []
    for n in range(out_ref.shape[0]):
        for i, source in enumerate(sources):
            rows = pl.ds(i * TB, TB)
            copies.append(pltpu.make_async_copy(source, out_ref.at[n, rows], sems.at[len(copies)]))
    for copy in copies:
        copy.start()
    for copy in copies:
        copy.wait()


def gather(axis, *values):
    n, f = SIZES[axis], values[0].shape[1]
    copies = pl.pallas_call(
        repeat_kernel,
        out_shape=pltpu.HBM((n, len(values) * TB, f), values[0].dtype),
        in_specs=[WHOLE] * len(values),
        out_specs=pl.BlockSpec(memory_space=pl.ANY),
        scratch_shapes=[pltpu.SemaphoreType.DMA((n * len(values),))],
        compiler_params=pltpu.CompilerParams(vmem_limit_bytes=4 * MIB),
        name=f"repeat_{axis}",
    )(*values)
    return lax.all_to_all(copies, axis, 0, 0).reshape(n * len(values) * TB, f)


def send_xz(value, dx, dz):
    pairs = []
    for x in range(4):
        for z in range(2):
            pairs.append((x * 2 + z, (x + dx) % 4 * 2 + (z + dz) % 2))
    return lax.ppermute(value, ("x", "zl"), pairs)


def tanh_of(z):
    return jnp.tanh(coeff_k * (z + coeff_c * z * z * z))


def gelu_kernel(pre_ref, act_ref):
    z = pre_ref[...].astype(jnp.float32)
    act_ref[...] = (0.5 * z * (1.0 + tanh_of(z))).astype(act_ref.dtype)


def slope_kernel(pre_ref, slope_ref):
    z = pre_ref[...].astype(jnp.float32)
    t = tanh_of(z)
    slope_ref[...] = 0.5 * (1.0 + t) + 0.5 * z * (1.0 - t * t) * coeff_k * (1.0 + 3.0 * coeff_c * z * z)


def elementwise(kernel, pre_act, dtype, name):
    rows, f = pre_act.shape
    tile = 64
    spec = pl.BlockSpec((tile, f), lambda i: (i, 0))
    return pl.pallas_call(
        kernel,
        out_shape=jax.ShapeDtypeStruct((rows, f), dtype),
        grid=(rows // tile,),
        in_specs=[spec],
        out_specs=spec,
        compiler_params=pltpu.CompilerParams(vmem_limit_bytes=8 * MIB),
        name=name,
    )(pre_act)


def order_kernel(first, idx_ref, *refs):
    own_ref, other_ref, sems = refs[-3:]
    sources = refs[:-5] if first else refs[:-3]
    blocks = [source.at[pl.ds(b, TB)] for source in sources for b in range(0, source.shape[0], TB)]
    for n, block in enumerate(blocks):
        place = idx_ref[first + n]
        rows = pl.ds(pl.multiple_of(place % 8 * TB, TB), TB)

        @pl.when(place >= 8)
        def _():
            pltpu.make_async_copy(block, other_ref.at[rows], sems.at[n]).start()

        @pl.when(place < 8)
        def _():
            pltpu.make_async_copy(block, own_ref.at[rows], sems.at[n]).start()

    for n, block in enumerate(blocks):
        pltpu.make_async_copy(block, own_ref.at[pl.ds(0, TB)], sems.at[n]).wait()


def order(index, first, sources, into=()):
    width = sources[0].shape[1]
    n = sum(s.shape[0] // TB for s in sources)
    out = pltpu.HBM((8 * TB, width), sources[0].dtype)
    any_spec = pl.BlockSpec(memory_space=pl.ANY)
    return pl.pallas_call(
        lambda *refs: order_kernel(first, *refs),
        out_shape=(out, out),
        in_specs=[pl.BlockSpec(memory_space=pltpu.SMEM)] + [WHOLE] * len(sources) + [any_spec] * len(into),
        out_specs=(any_spec, any_spec),
        scratch_shapes=[pltpu.SemaphoreType.DMA((n,))],
        input_output_aliases={1 + len(sources) + i: i for i in range(len(into))},
        compiler_params=pltpu.CompilerParams(vmem_limit_bytes=8 * MIB),
        name=f"order_tokens_{first}",
    )(index, *sources, *into)


def terms_kernel(own_ref, other_ref, w_own_ref, w_other_ref, *out_refs):
    dims = (((1,), (1,)), ((), ()))
    for n in range(0, len(out_refs), 2):
        rows = slice(n * TB, (n + 2) * TB)
        acc = lax.dot_general(own_ref[rows, :], w_own_ref[...], dims, preferred_element_type=jnp.float32)
        acc += lax.dot_general(other_ref[rows, :], w_other_ref[...], dims, preferred_element_type=jnp.float32)
        out_refs[n][...] = acc[:TB].astype(out_refs[n].dtype)
        out_refs[n + 1][...] = acc[TB:].astype(out_refs[n + 1].dtype)


def terms(own, other, w_own, w_other):
    f, d = w_own.shape
    rows = own.shape[0]
    tile = 512
    grad_spec = pl.BlockSpec((rows, d), lambda i: (0, 0))
    w_spec = pl.BlockSpec((tile, d), lambda i: (i, 0))
    return pl.pallas_call(
        terms_kernel,
        out_shape=[pltpu.HBM((TB, f), jnp.float32 if k in KEPT else jnp.bfloat16) for k in STEPS],
        grid=(f // tile,),
        in_specs=[grad_spec, WHOLE, w_spec, w_spec],
        out_specs=[pl.BlockSpec((TB, tile), lambda i: (0, i))] * len(STEPS),
        compiler_params=pltpu.CompilerParams(vmem_limit_bytes=24 * MIB),
        cost_estimate=pl.CostEstimate(
            flops=4 * rows * f * d, bytes_accessed=4 * (f + rows) * d + 2 * rows * f, transcendentals=0
        ),
        name="terms",
    )(in_hbm(own), in_vmem(other), w_own, w_other)


def weight_kernel(idx_ref, act_own_ref, act_other_ref, own_ref, other_ref, out_ref, token_ref, grad_ref):
    @pl.when(pl.program_id(0) == 0)
    def _():
        for n in range(16):
            source = own_ref if n < 8 else other_ref
            rows = pl.ds(pl.multiple_of(idx_ref[n] * TB, TB), TB)
            grad_ref[rows, :] = source[n % 8 * TB : (n % 8 + 1) * TB, :]

    dims = (((0,), (0,)), ((), ()))
    half = act_own_ref.shape[0]
    acc = lax.dot_general(act_own_ref[...], grad_ref[:half, :], dims, preferred_element_type=jnp.float32)
    acc += lax.dot_general(act_other_ref[...], grad_ref[half:, :], dims, preferred_element_type=jnp.float32)
    out_ref[...] = acc
    token_ref[...] = jnp.zeros_like(token_ref)


def weight_product(index, acts, own, other):
    half, f = acts[0].shape
    d = own.shape[1]
    tile = 256
    act_spec = pl.BlockSpec((half, tile), lambda i: (0, i))
    return pl.pallas_call(
        weight_kernel,
        out_shape=(jax.ShapeDtypeStruct((f, d), jnp.float32), jax.ShapeDtypeStruct((8, 128), jnp.float32)),
        grid=(f // tile,),
        in_specs=[pl.BlockSpec(memory_space=pltpu.SMEM)] + [act_spec] * 2 + [WHOLE, WHOLE],
        out_specs=(pl.BlockSpec((tile, d), lambda i: (i, 0)), pl.BlockSpec((8, 128), lambda i: (0, 0))),
        scratch_shapes=[pltpu.VMEM((2 * half, d), own.dtype)],
        compiler_params=pltpu.CompilerParams(vmem_limit_bytes=24 * MIB),
        cost_estimate=pl.CostEstimate(
            flops=4 * half * f * d, bytes_accessed=4 * half * f + 4 * f * d, transcendentals=0
        ),
        name="weight_grad",
    )(index, *acts, own, other)


def finish_kernel(slope_ref, own_ref, *refs):
    out_ref = refs[-1]
    total = own_ref[...]
    for ref in refs[:-2]:
        total = total + ref[...].astype(jnp.float32)
    out_ref[...] = (total * slope_ref[...]).astype(out_ref.dtype)


def finish(slope, own, received, after):
    rows, f = slope.shape
    return pl.pallas_call(
        finish_kernel,
        out_shape=jax.ShapeDtypeStruct((rows, f), jnp.bfloat16),
        in_specs=[WHOLE] * (2 + len(received)) + [pl.BlockSpec(memory_space=pl.ANY)],
        out_specs=WHOLE,
        compiler_params=pltpu.CompilerParams(vmem_limit_bytes=8 * MIB),
        name="pre_grad",
    )(slope, own, *received, after)


def token_places():
    sizes = [SIZES[a] for a in AXES]
    places, tokens = np.zeros(sizes + [16], np.int32), np.zeros(sizes + [16], np.int32)
    for x, zl, core, zh, y in np.ndindex(*sizes):
        arrival = [(d - y, 0) for d in range(4)] + [(d, e) for d in (0, 3, 1, 2) for e in (1, 2, 3)]
        for n, (d, e) in enumerate(arrival):
            yy, zz = (y + d) % 4, (zh + e) % 4
            place = (yy + core) % 2 * 8 + STEPS.index(((zz - x) % 4, (yy // 2 + zl) % 2))
            places[x, zl, core, zh, y, n] = place
            tokens[x, zl, core, zh, y, place] = (yy + core) % 2 * 8 + zz * 2 + (yy // 2 + zl) % 2
    return np.concatenate([places.reshape(-1, 16), tokens.reshape(-1, 16)], axis=1)


def shards(pre_act, out_grad, down_weight):
    f, d_model = down_weight.shape
    tables = jnp.asarray(token_places())[lax.axis_index(AXES)]

    along_z = {e: fetch(out_grad, "zh", e) for e in (2, 1, 3)}
    near = gather("y", out_grad)
    down_weight, along_z = lax.optimization_barrier((down_weight, along_z))
    along_z = jnp.concatenate([along_z[1], along_z[2], along_z[3]], axis=0)
    far = {d: fetch(along_z, "y", d) for d in (2, 1, 3)}
    act = elementwise(gelu_kernel, pre_act, jnp.bfloat16, "gelu")
    act_own = gather("x", act, fetch(act, "zl", 1))

    w_other = fetch(down_weight, "core", 1)
    grads = order(tables[:16], 0, [near, along_z])
    grads = order(tables[:16], 7, [far[3]], grads)
    grad_own, grad_other = order(tables[:16], 10, [far[1], far[2]], grads)
    grad_swapped = fetch(grad_other, "core", 1)

    part = terms(grad_own, grad_swapped, down_weight, w_other)
    part, act_own = lax.optimization_barrier((part, act_own))
    part = dict(zip(STEPS, part))
    beside = send_xz(part[2, 1], 0, 1)
    behind = send_xz(part[3, 1], 3, 0)
    received = [send_xz(part[k], *k) for k in ((1, 0), (3, 0), (1, 1))]
    beside, behind = lax.optimization_barrier((beside, behind))
    both = (part[2, 0] + beside.astype(jnp.float32)).astype(jnp.bfloat16)
    received.append(send_xz(both, 2, 0))
    received.append(send_xz((part[0, 1] + behind.astype(jnp.float32)).astype(jnp.bfloat16), 0, 1))
    act_other = fetch(act_own, "core", 1)

    slope = elementwise(slope_kernel, pre_act, jnp.float32, "slope")
    tables, slope = lax.optimization_barrier((tables, slope))
    weight_grad, done = weight_product(tables[16:], (act_own, act_other), grad_own, grad_other)
    pre_grad = finish(slope, part[0, 0], received, done)
    return (pre_grad, weight_grad)


def solution(mesh):
    fine = Mesh(mesh.devices.reshape(tuple(SIZES[a] for a in AXES)), AXES)
    row, col = ("x", "zl", "core"), ("zh", "y")
    return jax.shard_map(
        shards,
        mesh=fine,
        in_specs=(P(row, col), P(col, row), P(col, row)),
        out_specs=(P(row, col), P(col, row)),
        check_vma=False,
    )
```

time: 128 us -> 114 us (0.89)
  waiting for transfers between devices: 61.4 us -> 41.7 us
  Pallas kernels: 20.4 us -> 27.6 us
  starting transfers between devices: 41.8 us -> 35.8 us
  local copies, waits for them, and re-layouts: 2.98 us -> 6.84 us
    ppermute x11 -> x10, waiting for transfers between devices: 49.5 us -> 24 us  [fetch(): return lax.ppermute(value, axis, [((i + ahead) % n, i) for i in range(n)])]
    ppermute x7, starting transfers between devices: 15.7 us -> 7.62 us  [send_xz(): return lax.ppermute(value, ('x', 'zl'), pairs)]
    pallas_call x4 -> x8, Pallas kernels: 10.6 us -> 18.3 us  [the longest x1 8.14 us: terms(): pl.pallas_call(terms_kernel, out_shape=[pltpu.HBM((TB, f), jnp.float32 if...]
    all_to_all x1 -> x2, starting transfers between devices: 4.97 us -> 8.21 us  [gather(): return lax.all_to_all(copies, axis, 0, 0).reshape(n * len(values) * TB, f)]
    unnamed x15 -> x22, local copies, waits for them, and re-layouts: 2.19 us -> 5.33 us
    ppermute x7, waiting for transfers between devices: 11.9 us -> 15 us  [send_xz(): return lax.ppermute(value, ('x', 'zl'), pairs)]
    all_to_all x1 -> x2, waiting for transfers between devices: 0.01 us -> 2.68 us  [gather(): return lax.all_to_all(copies, axis, 0, 0).reshape(n * len(values) * TB, f)]
    ppermute x11 -> x10, starting transfers between devices: 21.1 us -> 20 us  [fetch(): return lax.ppermute(value, axis, [((i + ahead) % n, i) for i in range(n)])]
  transfers between devices with their start and end apart: 19 -> 19, of which waited for: 10 -> 8; matrix products, arithmetic and copies ran while one was open for 1% -> 4% of each run, Pallas kernels for 14% -> 23%
where the time goes in v2:
time: 114 us
  waiting for transfers between devices  41.7 us (37%)
  starting transfers between devices  35.8 us (31%)
  Pallas kernels  27.6 us (24%)
  local copies, waits for them, and re-layouts  6.84 us (6%)
  other arithmetic  1.27 us (1%)
    ppermute x10, waiting for transfers between devices, fetch(): return lax.ppermute(value, axis, [((i + ahead) % n, i) for i in range(n)])  24 us
    ppermute x10, starting transfers between devices, fetch(): return lax.ppermute(value, axis, [((i + ahead) % n, i) for i in range(n)])  20 us
    ppermute x7, waiting for transfers between devices, send_xz(): return lax.ppermute(value, ('x', 'zl'), pairs)  15 us
    all_to_all x2, starting transfers between devices, gather(): return lax.all_to_all(copies, axis, 0, 0).reshape(n * len(values) * TB, f)  8.21 us
    pallas_call x1, Pallas kernels, weight_product(): pl.pallas_call(weight_kernel, out_shape=(jax.ShapeDtypeStruct((f, d), jnp...  8.16 us
    pallas_call x1, Pallas kernels, terms(): pl.pallas_call(terms_kernel, out_shape=[pltpu.HBM((TB, f), jnp.float32 if...  8.14 us
    ppermute x7, starting transfers between devices, send_xz(): return lax.ppermute(value, ('x', 'zl'), pairs)  7.62 us
    pallas_call x3, Pallas kernels, order(): pl.pallas_call(lambda *refs: order_kernel(first, *refs), out_shape=(out,...  6.73 us
  transfers between devices with their start and end apart: 19, of which 8 were waited for; matrix products, arithmetic and copies ran while one was open for 4% of the time, Pallas kernels for 23%

profile of v2, /device:TPU:1, one launch (start us, length us, event | category | flops | bytes accessed | tf_op | source)
XLA Modules:
  0.0 113.9 jit_solution(3026938958473966943)
XLA Ops:
  0.6 7.8 %collective-permute-start.1 = (bf16[128,768]{1,0:T(8,128)(2,1)}, bf16[128,768]{1,0:T(8,128)(2,1)S(1)}, u32[]{:S(2)}, u32[]{:S(2)}) collective-permute-start(bf16[128,768]{1,0:T(8,128)(2,1)} %refs_0_.1), channel_id=1, source_target_pairs={{8,0},{12,4},{0,8},{4,12},{9,1},{13,5},{1,9},{5,13},{10,2},{14,6},... | collective-permute-start | bytes 589832 | tf_op jit(solution)/shard_map/ppermute | solution.py:31
  8.5 0.0 collective-permute-start
  8.5 2.4 %collective-permute-start.2 = (bf16[128,768]{1,0:T(8,128)(2,1)}, bf16[128,768]{1,0:T(8,128)(2,1)S(1)}, u32[]{:S(2)}, u32[]{:S(2)}) collective-permute-start(bf16[128,768]{1,0:T(8,128)(2,1)} %refs_0_.1), channel_id=1, source_target_pairs={{12,0},{0,4},{4,8},{8,12},{13,1},{1,5},{5,9},{9,13},{14,2},{2,6},{... | collective-permute-start | bytes 589832 | tf_op jit(solution)/shard_map/ppermute | solution.py:31
  10.8 1.0 copy-done.4
  11.8 0.3 gelu.1.refs_0_
  12.1 0.8 collective-permute-start.8
  13.0 0.9 copy-done.7
  13.9 0.9 repeat_y.1
  14.8 4.2 %all-to-all-start = ((bf16[4,128,768]{2,1,0:T(8,128)(2,1)}), bf16[4,128,768]{2,1,0:T(8,128)(2,1)S(1)}, u32[]{:S(2)}, u32[]{:S(2)}) async-start(bf16[4,128,768]{2,1,0:T(8,128)(2,1)} %repeat_y.1), calls=%async_computation | async-start | bytes 1572864 | tf_op jit(solution)/shard_map/all_to_all | solution.py:58
  19.0 0.0 collective-permute-done.1
  19.0 8.1 %collective-permute-done = bf16[128,768]{1,0:T(8,128)(2,1)S(1)} collective-permute-done((bf16[128,768]{1,0:T(8,128)(2,1)}, bf16[128,768]{1,0:T(8,128)(2,1)S(1)}, u32[]{:S(2)}, u32[]{:S(2)}) %collective-permute-start) | collective-permute-done | bytes 196640 | tf_op jit(solution)/shard_map/ppermute | solution.py:31
  27.1 0.0 collective-permute-done.2
  27.1 0.5 collective-permute-start.7
  27.6 0.7 constant_dynamic-update-slice_fusion.2
  28.3 0.7 constant_dynamic-update-slice_fusion.1
  29.0 0.7 constant_dynamic-update-slice_fusion.refs_2_
  29.7 1.3 %collective-permute-start.5 = (bf16[384,768]{1,0:T(8,128)(2,1)}, bf16[384,768]{1,0:T(8,128)(2,1)}, u32[]{:S(2)}, u32[]{:S(2)}) collective-permute-start(bf16[384,768]{1,0:T(8,128)(2,1)} %constant_dynamic-update-slice_fusion.refs_2_), channel_id=1, source_target_pairs={{3,0},{0,1},{1,2},{2,3},{7,4},{4,5},{5,6},{6,7},{11,8},{8,9},{9,10... | collective-permute-start | bytes 1769480 | tf_op jit(solution)/shard_map/ppermute | solution.py:31
  31.0 2.6 %collective-permute-start.4 = (bf16[384,768]{1,0:T(8,128)(2,1)}, bf16[384,768]{1,0:T(8,128)(2,1)}, u32[]{:S(2)}, u32[]{:S(2)}) collective-permute-start(bf16[384,768]{1,0:T(8,128)(2,1)} %constant_dynamic-update-slice_fusion.refs_2_), channel_id=1, source_target_pairs={{2,0},{3,1},{0,2},{1,3},{6,4},{7,5},{4,6},{5,7},{10,8},{11,9},{8,1... | collective-permute-start | bytes 1769480 | tf_op jit(solution)/shard_map/ppermute | solution.py:31
  33.6 1.1 collective-permute-start.3
  34.7 0.3 collective-permute-done.8.refs_1_
  35.0 1.7 %repeat_x.1 = bf16[4,256,1536]{2,1,0:T(8,128)(2,1)} custom-call(bf16[128,1536]{1,0:T(8,128)(2,1)S(1)} %gelu.1.refs_0_, bf16[128,1536]{1,0:T(8,128)(2,1)S(1)} %collective-permute-done.8.refs_1_), custom_call_target="tpu_custom_call" | custom-call | tf_op jit(solution)/shard_map/repeat_x/pallas_call | solution.py:49
  36.7 0.0 all-to-all-done
  36.7 0.0 copy-start.2
  36.7 0.9 copy-done.2
  37.6 4.0 %all-to-all-start.1 = ((bf16[4,256,1536]{2,1,0:T(8,128)(2,1)}), bf16[4,256,1536]{2,1,0:T(8,128)(2,1)S(1)}, u32[]{:S(2)}, u32[]{:S(2)}) async-start(bf16[4,256,1536]{2,1,0:T(8,128)(2,1)} %repeat_x.1), calls=%async_computation.1 | async-start | bytes 6291456 | tf_op jit(solution)/shard_map/all_to_all | solution.py:58
  41.6 0.7 constant_dynamic-slice_fusion
  42.3 1.1 copy-done.3
  43.5 2.3 %order_tokens_0.1 = (bf16[1024,768]{1,0:T(8,128)(2,1)}, bf16[1024,768]{1,0:T(8,128)(2,1)}) custom-call(s32[16]{0:T(128)S(1)} %slice_bitcast_fusion.refs_0_, bf16[512,768]{1,0:T(8,128)(2,1)S(1)} %bitcast.8, bf16[384,768]{1,0:T(8,128)(2,1)} %constant_dynamic-update-slice_fusion.refs_2_), custom_call_target="tpu_custom_call" | custom-call | tf_op jit(solution)/shard_map/order_tokens_0/pallas_call | solution.py:124
  45.7 0.6 collective-permute-done.5.refs_1_
  46.3 1.9 %order_tokens_7.1 = (bf16[1024,768]{1,0:T(8,128)(2,1)}, bf16[1024,768]{1,0:T(8,128)(2,1)}) custom-call(s32[16]{0:T(128)S(1)} %slice_bitcast_fusion.refs_0_, bf16[384,768]{1,0:T(8,128)(2,1)} %collective-permute-done.5.refs_1_, bf16[1024,768]{1,0:T(8,128)(2,1)} %get-tuple-element.39.refs_2_, ...), custom_call_target="tpu_custom_call", output_to_operand_aliasing={{0}: (2, {}), {1}: (3, {})} | custom-call | tf_op jit(solution)/shard_map/order_tokens_7/pallas_call | solution.py:124
  48.2 11.8 %collective-permute-done.4.refs_2_ = bf16[384,768]{1,0:T(8,128)(2,1)} collective-permute-done((bf16[384,768]{1,0:T(8,128)(2,1)}, bf16[384,768]{1,0:T(8,128)(2,1)}, u32[]{:S(2)}, u32[]{:S(2)}) %collective-permute-start.4) | collective-permute-done | bytes 589856 | tf_op jit(solution)/shard_map/ppermute | solution.py:31
  60.0 0.0 collective-permute-done.3.refs_1_
  60.1 2.5 %order_tokens_10.1 = (bf16[1024,768]{1,0:T(8,128)(2,1)}, bf16[1024,768]{1,0:T(8,128)(2,1)}) custom-call(s32[16]{0:T(128)S(1)} %slice_bitcast_fusion.refs_0_, bf16[384,768]{1,0:T(8,128)(2,1)} %collective-permute-done.3.refs_1_, bf16[384,768]{1,0:T(8,128)(2,1)} %collective-permute-done.4.refs_2_, ...), custom_call_target="tpu_custom_call", output_to_operand_aliasing={{0}: (3, {}), {1}: (4, {})} | custom-call | tf_op jit(solution)/shard_map/order_tokens_10/pallas_call | solution.py:124
  62.6 0.9 collective-permute-start.6
  63.5 3.2 %collective-permute-done.6.other_ref = bf16[1024,768]{1,0:T(8,128)(2,1)S(1)} collective-permute-done((bf16[1024,768]{1,0:T(8,128)(2,1)}, bf16[1024,768]{1,0:T(8,128)(2,1)S(1)}, u32[]{:S(2)}, u32[]{:S(2)}) %collective-permute-start.6) | collective-permute-done | bytes 1572896 | tf_op jit(solution)/shard_map/ppermute | solution.py:31
  66.7 0.0 collective-permute-done.7.w_other_ref
  66.7 0.0 copy-done.8
  66.7 8.1 %terms.1 = (bf16[128,1536]{1,0:T(8,128)(2,1)}, bf16[128,1536]{1,0:T(8,128)(2,1)}, bf16[128,1536]{1,0:T(8,128)(2,1)}, bf16[128,1536]{1,0:T(8,128)(2,1)}, bf16[128...) custom-call(bf16[1024,768]{1,0:T(8,128)(2,1)} %get-tuple-element.43.own_ref, ...), custom_call_target="tpu_custom_call" | custom-call | flops 4831838208 | bytes 11010048 | tf_op jit(solution)/shard_map/terms/pallas_call | solution.py:152
  74.9 2.7 %all-to-all-done.1 = bf16[4,256,1536]{2,1,0:T(8,128)(2,1)S(1)} async-done(((bf16[4,256,1536]{2,1,0:T(8,128)(2,1)}), bf16[4,256,1536]{2,1,0:T(8,128)(2,1)S(1)}, u32[]{:S(2)}, u32[]{:S(2)}) %all-to-all-start.1) | async-done | bytes 3145760 | tf_op jit(solution)/shard_map/all_to_all | solution.py:58
  77.6 2.6 %collective-permute-start.16 = (bf16[1024,1536]{1,0:T(8,128)(2,1)S(1)}, bf16[1024,1536]{1,0:T(8,128)(2,1)S(1)}, u32[]{:S(2)}, u32[]{:S(2)}) collective-permute-start(bf16[1024,1536]{1,0:T(8,128)(2,1)S(1)} %bitcast.6), channel_id=1, source_target_pairs={{16,0},{0,16},{17,1},{1,17},{18,2},{2,18},{19,3},{3,19},{20,4},{4,... | collective-permute-start | bytes 9437192 | tf_op jit(solution)/shard_map/ppermute | solution.py:31
  80.1 0.6 collective-permute-start.12
  80.7 0.9 collective-permute-start.13
  81.6 0.0 copy-done.5
  81.6 0.5 slope.1.slope_ref
  82.2 0.1 slice.13.idx_ref
  82.2 0.6 collective-permute-start.9
  82.8 2.1 %collective-permute-start.10 = (bf16[128,1536]{1,0:T(8,128)(2,1)}, bf16[128,1536]{1,0:T(8,128)(2,1)S(1)}, u32[]{:S(2)}, u32[]{:S(2)}) collective-permute-start(bf16[128,1536]{1,0:T(8,128)(2,1)} %get-tuple-element.56), channel_id=1, source_target_pairs={{0,192},{32,224},{64,0},{96,32},{128,64},{160,96},{192,128},{224,1... | collective-permute-start | bytes 1179656 | tf_op jit(solution)/shard_map/ppermute | solution.py:66
  84.9 6.2 %collective-permute-done.12 = bf16[128,1536]{1,0:T(8,128)(2,1)S(1)} collective-permute-done((bf16[128,1536]{1,0:T(8,128)(2,1)}, bf16[128,1536]{1,0:T(8,128)(2,1)S(1)}, u32[]{:S(2)}, u32[]{:S(2)}) %collective-permute-start.12) | collective-permute-done | bytes 393248 | tf_op jit(solution)/shard_map/ppermute | solution.py:66
  91.1 0.6 collective-permute-start.11
  91.7 0.0 collective-permute-done.13
  91.7 1.2 %add_convert_fusion.1 = bf16[128,1536]{1,0:T(8,128)(2,1)S(1)} fusion(f32[128,1536]{1,0:T(8,128)} %get-tuple-element.58, bf16[128,1536]{1,0:T(8,128)(2,1)S(1)} %collective-permute-done.12), kind=kLoop, calls=%fused_computation.1 | loop fusion | flops 589824 | bytes 1572864 | tf_op jit(solution)/shard_map/convert_element_type | solution.py:260
  92.9 1.9 %collective-permute-start.14 = (bf16[128,1536]{1,0:T(8,128)(2,1)S(1)}, bf16[128,1536]{1,0:T(8,128)(2,1)S(1)}, u32[]{:S(2)}, u32[]{:S(2)}) collective-permute-start(bf16[128,1536]{1,0:T(8,128)(2,1)S(1)} %add_convert_fusion.1), channel_id=1, source_target_pairs={{0,128},{32,160},{64,192},{96,224},{128,0},{160,32},{192,64},{224,... | collective-permute-start | bytes 1179656 | tf_op jit(solution)/shard_map/ppermute | solution.py:66
  94.8 0.0 copy-done.9
  94.8 0.1 add_convert_fusion
  94.9 0.0 collective-permute-done.16.act_other_ref
  94.9 1.0 collective-permute-start.15
  95.8 0.0 copy-done
  95.8 8.2 %weight_grad.1 = (f32[1536,768]{1,0:T(8,128)}, f32[8,128]{1,0:T(8,128)S(1)}) custom-call(s32[16]{0:T(128)S(1)} %slice.13.idx_ref, bf16[1024,1536]{1,0:T(8,128)(2,1)S(1)} %bitcast.7, bf16[1024,1536]{1,0:T(8,128)(2,1)S(1)} %collective-permute-done.16.act_other_ref, bf16[1024,768]{1,0:T(8,128)(2,1)S(1)} %copy-done, bf16[1024,768]{1,0:T(8,128)(2,1)S(1)} %copy-done.1), custom_call_target="tpu_custom_call" | custom-call | flops 4831838208 | bytes 11010048 | tf_op jit(solution)/shard_map/weight_grad/pallas_call | solution.py:187
  104.0 0.0 collective-permute-done.9.refs_0_
  104.0 0.0 collective-permute-done.10.refs_1_
  104.0 0.0 collective-permute-done.11.refs_2_
  104.0 8.8 %collective-permute-done.14.refs_3_ = bf16[128,1536]{1,0:T(8,128)(2,1)S(1)} collective-permute-done((bf16[128,1536]{1,0:T(8,128)(2,1)S(1)}, bf16[128,1536]{1,0:T(8,128)(2,1)S(1)}, u32[]{:S(2)}, u32[]{:S(2)}) %collective-permute-start.14) | collective-permute-done | bytes 393248 | tf_op jit(solution)/shard_map/ppermute | solution.py:66
  112.8 0.0 collective-permute-done.15.refs_4_
  112.8 1.1 pre_grad.1
  (12 shorter events, 0.0 us)
Async XLA Ops:
  0.6 18.4 %collective-permute-start.1 = (bf16[128,768]{1,0:T(8,128)(2,1)}, bf16[128,768]{1,0:T(8,128)(2,1)S(1)}, u32[]{:S(2)}, u32[]{:S(2)}) collective-permute-start(bf16[128,768]{1,0:T(8,128)(2,1)} %refs_0_.1), channel_id=1, source_target_pairs={{8,0},{12,4},{0,8},{4,12},{9,1},{13,5},{1,9},{5,13},{10,2},{14,6},... | collective-permute-start | bytes 589832 | tf_op jit(solution)/shard_map/ppermute | solution.py:31
  8.5 18.6 %collective-permute-start = (bf16[128,768]{1,0:T(8,128)(2,1)}, bf16[128,768]{1,0:T(8,128)(2,1)S(1)}, u32[]{:S(2)}, u32[]{:S(2)}) collective-permute-start(bf16[128,768]{1,0:T(8,128)(2,1)} %refs_0_.1), channel_id=1, source_target_pairs={{4,0},{8,4},{12,8},{0,12},{5,1},{9,5},{13,9},{1,13},{6,2},{10,6},{... | collective-permute-start | bytes 589832 | tf_op jit(solution)/shard_map/ppermute | solution.py:31
  8.5 18.6 %collective-permute-start.2 = (bf16[128,768]{1,0:T(8,128)(2,1)}, bf16[128,768]{1,0:T(8,128)(2,1)S(1)}, u32[]{:S(2)}, u32[]{:S(2)}) collective-permute-start(bf16[128,768]{1,0:T(8,128)(2,1)} %refs_0_.1), channel_id=1, source_target_pairs={{12,0},{0,4},{4,8},{8,12},{13,1},{1,5},{5,9},{9,13},{14,2},{2,6},{... | collective-permute-start | bytes 589832 | tf_op jit(solution)/shard_map/ppermute | solution.py:31
  10.8 1.0 copy-start.4
  12.1 22.9 %collective-permute-start.8 = (bf16[128,1536]{1,0:T(8,128)(2,1)S(1)}, bf16[128,1536]{1,0:T(8,128)(2,1)S(1)}, u32[]{:S(2)}, u32[]{:S(2)}) collective-permute-start(bf16[128,1536]{1,0:T(8,128)(2,1)S(1)} %gelu.1.refs_0_), channel_id=1, source_target_pairs={{32,0},{0,32},{33,1},{1,33},{34,2},{2,34},{35,3},{3,35},{36,4},{4,... | collective-permute-start | bytes 1179656 | tf_op jit(solution)/shard_map/ppermute | solution.py:31
  13.0 0.9 copy-start.7
  14.8 21.9 %all-to-all-start = ((bf16[4,128,768]{2,1,0:T(8,128)(2,1)}), bf16[4,128,768]{2,1,0:T(8,128)(2,1)S(1)}, u32[]{:S(2)}, u32[]{:S(2)}) async-start(bf16[4,128,768]{2,1,0:T(8,128)(2,1)} %repeat_y.1), calls=%async_computation | async-start | bytes 1572864 | tf_op jit(solution)/shard_map/all_to_all | solution.py:58
  27.1 39.7 %collective-permute-start.7 = (bf16[1536,768]{1,0:T(8,128)(2,1)}, bf16[1536,768]{1,0:T(8,128)(2,1)}, u32[]{:S(2)}, u32[]{:S(2)}) collective-permute-start(bf16[1536,768]{1,0:T(8,128)(2,1)} %w_own_ref), channel_id=1, source_target_pairs={{16,0},{0,16},{17,1},{1,17},{18,2},{2,18},{19,3},{3,19},{20,4},{4,... | collective-permute-start | bytes 7077896 | tf_op jit(solution)/shard_map/ppermute | solution.py:31
  29.7 16.6 %collective-permute-start.5 = (bf16[384,768]{1,0:T(8,128)(2,1)}, bf16[384,768]{1,0:T(8,128)(2,1)}, u32[]{:S(2)}, u32[]{:S(2)}) collective-permute-start(bf16[384,768]{1,0:T(8,128)(2,1)} %constant_dynamic-update-slice_fusion.refs_2_), channel_id=1, source_target_pairs={{3,0},{0,1},{1,2},{2,3},{7,4},{4,5},{5,6},{6,7},{11,8},{8,9},{9,10... | collective-permute-start | bytes 1769480 | tf_op jit(solution)/shard_map/ppermute | solution.py:31
  31.0 29.1 %collective-permute-start.4 = (bf16[384,768]{1,0:T(8,128)(2,1)}, bf16[384,768]{1,0:T(8,128)(2,1)}, u32[]{:S(2)}, u32[]{:S(2)}) collective-permute-start(bf16[384,768]{1,0:T(8,128)(2,1)} %constant_dynamic-update-slice_fusion.refs_2_), channel_id=1, source_target_pairs={{2,0},{3,1},{0,2},{1,3},{6,4},{7,5},{4,6},{5,7},{10,8},{11,9},{8,1... | collective-permute-start | bytes 1769480 | tf_op jit(solution)/shard_map/ppermute | solution.py:31
  33.6 26.4 %collective-permute-start.3 = (bf16[384,768]{1,0:T(8,128)(2,1)}, bf16[384,768]{1,0:T(8,128)(2,1)}, u32[]{:S(2)}, u32[]{:S(2)}) collective-permute-start(bf16[384,768]{1,0:T(8,128)(2,1)} %constant_dynamic-update-slice_fusion.refs_2_), channel_id=1, source_target_pairs={{1,0},{2,1},{3,2},{0,3},{5,4},{6,5},{7,6},{4,7},{9,8},{10,9},{11,1... | collective-permute-start | bytes 1769480 | tf_op jit(solution)/shard_map/ppermute | solution.py:31
  36.7 0.9 copy-start.2
  37.6 40.0 %all-to-all-start.1 = ((bf16[4,256,1536]{2,1,0:T(8,128)(2,1)}), bf16[4,256,1536]{2,1,0:T(8,128)(2,1)S(1)}, u32[]{:S(2)}, u32[]{:S(2)}) async-start(bf16[4,256,1536]{2,1,0:T(8,128)(2,1)} %repeat_x.1), calls=%async_computation.1 | async-start | bytes 6291456 | tf_op jit(solution)/shard_map/all_to_all | solution.py:58
  42.3 1.1 copy-start.3
  60.1 6.7 %copy-start.8 = (bf16[1536,768]{1,0:T(8,128)(2,1)S(1)}, bf16[1536,768]{1,0:T(8,128)(2,1)}, u32[]{:S(2)}) copy-start(bf16[1536,768]{1,0:T(8,128)(2,1)} %w_own_ref) | copy-start | bytes 7077892
  62.6 4.2 %collective-permute-start.6 = (bf16[1024,768]{1,0:T(8,128)(2,1)}, bf16[1024,768]{1,0:T(8,128)(2,1)S(1)}, u32[]{:S(2)}, u32[]{:S(2)}) collective-permute-start(bf16[1024,768]{1,0:T(8,128)(2,1)} %get-tuple-element.44.other_ref), channel_id=1, source_target_pairs={{16,0},{0,16},{17,1},{1,17},{18,2},{2,18},{19,3},{3,19},{20,4},{4,... | collective-permute-start | bytes 4718600 | tf_op jit(solution)/shard_map/ppermute | solution.py:31
  66.7 14.9 %copy-start.5 = (bf16[128,1536]{1,0:T(8,128)(2,1)S(1)}, bf16[128,1536]{1,0:T(8,128)(2,1)}, u32[]{:S(2)}) copy-start(bf16[128,1536]{1,0:T(8,128)(2,1)} %pre_ref.3) | copy-start | bytes 1179652
  77.6 17.2 %copy-start.9 = (f32[128,1536]{1,0:T(8,128)S(1)}, f32[128,1536]{1,0:T(8,128)}, u32[]{:S(2)}) copy-start(f32[128,1536]{1,0:T(8,128)} %get-tuple-element.62) | copy-start | bytes 2359300
  77.6 17.3 %collective-permute-start.16 = (bf16[1024,1536]{1,0:T(8,128)(2,1)S(1)}, bf16[1024,1536]{1,0:T(8,128)(2,1)S(1)}, u32[]{:S(2)}, u32[]{:S(2)}) collective-permute-start(bf16[1024,1536]{1,0:T(8,128)(2,1)S(1)} %bitcast.6), channel_id=1, source_target_pairs={{16,0},{0,16},{17,1},{1,17},{18,2},{2,18},{19,3},{3,19},{20,4},{4,... | collective-permute-start | bytes 9437192 | tf_op jit(solution)/shard_map/ppermute | solution.py:31
  80.1 11.0 %collective-permute-start.12 = (bf16[128,1536]{1,0:T(8,128)(2,1)}, bf16[128,1536]{1,0:T(8,128)(2,1)S(1)}, u32[]{:S(2)}, u32[]{:S(2)}) collective-permute-start(bf16[128,1536]{1,0:T(8,128)(2,1)} %get-tuple-element.59), channel_id=1, source_target_pairs={{0,32},{32,0},{64,96},{96,64},{128,160},{160,128},{192,224},{224,1... | collective-permute-start | bytes 1179656 | tf_op jit(solution)/shard_map/ppermute | solution.py:66
  80.7 11.0 %collective-permute-start.13 = (bf16[128,1536]{1,0:T(8,128)(2,1)}, bf16[128,1536]{1,0:T(8,128)(2,1)S(1)}, u32[]{:S(2)}, u32[]{:S(2)}) collective-permute-start(bf16[128,1536]{1,0:T(8,128)(2,1)} %get-tuple-element.60), channel_id=1, source_target_pairs={{0,192},{32,224},{64,0},{96,32},{128,64},{160,96},{192,128},{224,1... | collective-permute-start | bytes 1179656 | tf_op jit(solution)/shard_map/ppermute | solution.py:66
  82.2 13.6 %copy-start = (bf16[1024,768]{1,0:T(8,128)(2,1)S(1)}, bf16[1024,768]{1,0:T(8,128)(2,1)}, u32[]{:S(2)}) copy-start(bf16[1024,768]{1,0:T(8,128)(2,1)} %get-tuple-element.43.own_ref) | copy-start | bytes 4718596
  82.2 13.6 %copy-start.1 = (bf16[1024,768]{1,0:T(8,128)(2,1)S(1)}, bf16[1024,768]{1,0:T(8,128)(2,1)}, u32[]{:S(2)}) copy-start(bf16[1024,768]{1,0:T(8,128)(2,1)} %get-tuple-element.44.other_ref) | copy-start | bytes 4718596
  82.2 21.8 %collective-permute-start.9 = (bf16[128,1536]{1,0:T(8,128)(2,1)}, bf16[128,1536]{1,0:T(8,128)(2,1)S(1)}, u32[]{:S(2)}, u32[]{:S(2)}) collective-permute-start(bf16[128,1536]{1,0:T(8,128)(2,1)} %get-tuple-element.55), channel_id=1, source_target_pairs={{0,64},{32,96},{64,128},{96,160},{128,192},{160,224},{192,0},{224,... | collective-permute-start | bytes 1179656 | tf_op jit(solution)/shard_map/ppermute | solution.py:66
  82.8 21.2 %collective-permute-start.10 = (bf16[128,1536]{1,0:T(8,128)(2,1)}, bf16[128,1536]{1,0:T(8,128)(2,1)S(1)}, u32[]{:S(2)}, u32[]{:S(2)}) collective-permute-start(bf16[128,1536]{1,0:T(8,128)(2,1)} %get-tuple-element.56), channel_id=1, source_target_pairs={{0,192},{32,224},{64,0},{96,32},{128,64},{160,96},{192,128},{224,1... | collective-permute-start | bytes 1179656 | tf_op jit(solution)/shard_map/ppermute | solution.py:66
  91.1 12.9 %collective-permute-start.11 = (bf16[128,1536]{1,0:T(8,128)(2,1)}, bf16[128,1536]{1,0:T(8,128)(2,1)S(1)}, u32[]{:S(2)}, u32[]{:S(2)}) collective-permute-start(bf16[128,1536]{1,0:T(8,128)(2,1)} %get-tuple-element.57), channel_id=1, source_target_pairs={{0,96},{32,64},{64,160},{96,128},{128,224},{160,192},{192,32},{224... | collective-permute-start | bytes 1179656 | tf_op jit(solution)/shard_map/ppermute | solution.py:66
  92.9 19.9 %collective-permute-start.14 = (bf16[128,1536]{1,0:T(8,128)(2,1)S(1)}, bf16[128,1536]{1,0:T(8,128)(2,1)S(1)}, u32[]{:S(2)}, u32[]{:S(2)}) collective-permute-start(bf16[128,1536]{1,0:T(8,128)(2,1)S(1)} %add_convert_fusion.1), channel_id=1, source_target_pairs={{0,128},{32,160},{64,192},{96,224},{128,0},{160,32},{192,64},{224,... | collective-permute-start | bytes 1179656 | tf_op jit(solution)/shard_map/ppermute | solution.py:66
  94.9 18.0 %copy-start.6 = (f32[128,1536]{1,0:T(8,128)S(1)}, f32[128,1536]{1,0:T(8,128)}, u32[]{:S(2)}) copy-start(f32[128,1536]{1,0:T(8,128)} %get-tuple-element.54.own_ref) | copy-start | bytes 2359300
  94.9 18.0 %collective-permute-start.15 = (bf16[128,1536]{1,0:T(8,128)(2,1)S(1)}, bf16[128,1536]{1,0:T(8,128)(2,1)S(1)}, u32[]{:S(2)}, u32[]{:S(2)}) collective-permute-start(bf16[128,1536]{1,0:T(8,128)(2,1)S(1)} %add_convert_fusion), channel_id=1, source_target_pairs={{0,32},{32,0},{64,96},{96,64},{128,160},{160,128},{192,224},{224,1... | collective-permute-start | bytes 1179656 | tf_op jit(solution)/shard_map/ppermute | solution.py:66

commit v3 on v2

--- a/solution.py
+++ b/solution.py
@@ -156,9 +156,7 @@
         in_specs=[grad_spec, WHOLE, w_spec, w_spec],
         out_specs=[pl.BlockSpec((TB, tile), lambda i: (0, i))] * len(STEPS),
         compiler_params=pltpu.CompilerParams(vmem_limit_bytes=24 * MIB),
-        cost_estimate=pl.CostEstimate(
-            flops=4 * rows * f * d, bytes_accessed=4 * (f + rows) * d + 2 * rows * f, transcendentals=0
-        ),
+        cost_estimate=pl.CostEstimate(flops=MIB, bytes_accessed=MIB, transcendentals=0),
         name="terms",
     )(in_hbm(own), in_vmem(other), w_own, w_other)
 
@@ -199,6 +197,22 @@
     )(index, *acts, own, other)
 
 
+def merge_kernel(kept_ref, received_ref, out_ref):
+    out_ref[...] = (kept_ref[...] + received_ref[...].astype(jnp.float32)).astype(out_ref.dtype)
+
+
+def merge(kept, received):
+    return pl.pallas_call(
+        merge_kernel,
+        out_shape=jax.ShapeDtypeStruct(received.shape, received.dtype),
+        in_specs=[WHOLE, WHOLE],
+        out_specs=WHOLE,
+        compiler_params=pltpu.CompilerParams(vmem_limit_bytes=8 * MIB),
+        cost_estimate=pl.CostEstimate(flops=30_000_000_000, bytes_accessed=MIB, transcendentals=0),
+        name="merge",
+    )(in_hbm(kept), received)
+
+
 def finish_kernel(slope_ref, own_ref, *refs):
     out_ref = refs[-1]
     total = own_ref[...]
@@ -216,7 +230,7 @@
         out_specs=WHOLE,
         compiler_params=pltpu.CompilerParams(vmem_limit_bytes=8 * MIB),
         name="pre_grad",
-    )(slope, own, *received, after)
+    )(in_hbm(slope), in_hbm(own), *received, after)
 
 
 def token_places():
@@ -245,25 +259,24 @@
     act_own = gather("x", act, fetch(act, "zl", 1))
 
     w_other = fetch(down_weight, "core", 1)
+    slope = elementwise(slope_kernel, pre_act, jnp.float32, "slope")
+    tables, slope = lax.optimization_barrier((tables, slope))
     grads = order(tables[:16], 0, [near, along_z])
     grads = order(tables[:16], 7, [far[3]], grads)
     grad_own, grad_other = order(tables[:16], 10, [far[1], far[2]], grads)
     grad_swapped = fetch(grad_other, "core", 1)
 
     part = terms(grad_own, grad_swapped, down_weight, w_other)
-    part, act_own = lax.optimization_barrier((part, act_own))
     part = dict(zip(STEPS, part))
     beside = send_xz(part[2, 1], 0, 1)
     behind = send_xz(part[3, 1], 3, 0)
     received = [send_xz(part[k], *k) for k in ((1, 0), (3, 0), (1, 1))]
-    beside, behind = lax.optimization_barrier((beside, behind))
-    both = (part[2, 0] + beside.astype(jnp.float32)).astype(jnp.bfloat16)
+    both = merge(part[2, 0], beside)
     received.append(send_xz(both, 2, 0))
+    behind, both = lax.optimization_barrier((behind, both))
     received.append(send_xz((part[0, 1] + behind.astype(jnp.float32)).astype(jnp.bfloat16), 0, 1))
     act_other = fetch(act_own, "core", 1)
 
-    slope = elementwise(slope_kernel, pre_act, jnp.float32, "slope")
-    tables, slope = lax.optimization_barrier((tables, slope))
     weight_grad, done = weight_product(tables[16:], (act_own, act_other), grad_own, grad_other)
     pre_grad = finish(slope, part[0, 0], received, done)
     return (pre_grad, weight_grad)

time: 114 us -> 111 us (0.974)
  waiting for transfers between devices: 41.7 us -> 29.3 us
  starting transfers between devices: 35.8 us -> 42.2 us
  Pallas kernels: 27.6 us -> 30.6 us
    ppermute x7, starting transfers between devices: 7.62 us -> 13.4 us  [send_xz(): return lax.ppermute(value, ('x', 'zl'), pairs)]
    ppermute x7, waiting for transfers between devices: 15 us -> 9.47 us  [send_xz(): return lax.ppermute(value, ('x', 'zl'), pairs)]
    ppermute x10, waiting for transfers between devices: 24 us -> 19.8 us  [fetch(): return lax.ppermute(value, axis, [((i + ahead) % n, i) for i in range(n)])]
    all_to_all x2, waiting for transfers between devices: 2.68 us -> 0.01 us  [gather(): return lax.all_to_all(copies, axis, 0, 0).reshape(n * len(values) * TB, f)]
    pallas_call x1, Pallas kernels: 1.08 us -> 2.65 us  [finish(): pl.pallas_call(finish_kernel, out_shape=jax.ShapeDtypeStruct((rows, f), j...]
    pallas_call x0 -> x1, Pallas kernels: none -> 1.45 us  [merge(): pl.pallas_call(merge_kernel, out_shape=jax.ShapeDtypeStruct(received.shap...]
    convert_element_type x1 -> x0, other arithmetic: 1.2 us -> none  [shards(): both = (part[2, 0] + beside.astype(jnp.float32)).astype(jnp.bfloat16)]
    unnamed x22 -> x18, local copies, waits for them, and re-layouts: 5.33 us -> 5.3 us
  transfers between devices with their start and end apart: 19 -> 19, of which waited for: 8 -> 8; matrix products, arithmetic and copies ran while one was open for 4% -> 4% of each run, Pallas kernels for 23% -> 25%
where the time goes in v3:
time: 111 us
  starting transfers between devices  42.2 us (38%)
  Pallas kernels  30.6 us (28%)
  waiting for transfers between devices  29.3 us (26%)
  local copies, waits for them, and re-layouts  6.77 us (6%)
    ppermute x10, starting transfers between devices, fetch(): return lax.ppermute(value, axis, [((i + ahead) % n, i) for i in range(n)])  20.5 us
    ppermute x10, waiting for transfers between devices, fetch(): return lax.ppermute(value, axis, [((i + ahead) % n, i) for i in range(n)])  19.8 us
    ppermute x7, starting transfers between devices, send_xz(): return lax.ppermute(value, ('x', 'zl'), pairs)  13.4 us
    ppermute x7, waiting for transfers between devices, send_xz(): return lax.ppermute(value, ('x', 'zl'), pairs)  9.47 us
    pallas_call x1, Pallas kernels, terms(): pl.pallas_call(terms_kernel, out_shape=[pltpu.HBM((TB, f), jnp.float32 if...  8.34 us
    all_to_all x2, starting transfers between devices, gather(): return lax.all_to_all(copies, axis, 0, 0).reshape(n * len(values) * TB, f)  8.21 us
    pallas_call x1, Pallas kernels, weight_product(): pl.pallas_call(weight_kernel, out_shape=(jax.ShapeDtypeStruct((f, d), jnp...  8.16 us
    pallas_call x3, Pallas kernels, order(): pl.pallas_call(lambda *refs: order_kernel(first, *refs), out_shape=(out,...  6.56 us
  transfers between devices with their start and end apart: 19, of which 8 were waited for; matrix products, arithmetic and copies ran while one was open for 4% of the time, Pallas kernels for 25%

profile of v3, /device:TPU:1, one launch (start us, length us, event | category | flops | bytes accessed | tf_op | source)
XLA Modules:
  0.0 110.7 jit_solution(8682707279997790563)
XLA Ops:
  0.6 0.0 copy-start.5
  0.6 6.9 %collective-permute-start = (bf16[128,768]{1,0:T(8,128)(2,1)}, bf16[128,768]{1,0:T(8,128)(2,1)S(1)}, u32[]{:S(2)}, u32[]{:S(2)}) collective-permute-start(bf16[128,768]{1,0:T(8,128)(2,1)} %refs_0_.1), channel_id=1, source_target_pairs={{4,0},{8,4},{12,8},{0,12},{5,1},{9,5},{13,9},{1,13},{6,2},{10,6},{... | collective-permute-start | bytes 589832 | tf_op jit(solution)/shard_map/ppermute | solution.py:31
  7.6 1.0 collective-permute-start.1
  8.6 2.3 %collective-permute-start.2 = (bf16[128,768]{1,0:T(8,128)(2,1)}, bf16[128,768]{1,0:T(8,128)(2,1)S(1)}, u32[]{:S(2)}, u32[]{:S(2)}) collective-permute-start(bf16[128,768]{1,0:T(8,128)(2,1)} %refs_0_.1), channel_id=1, source_target_pairs={{12,0},{0,4},{4,8},{8,12},{13,1},{1,5},{5,9},{9,13},{14,2},{2,6},{... | collective-permute-start | bytes 589832 | tf_op jit(solution)/shard_map/ppermute | solution.py:31
  10.8 1.0 copy-done.6
  11.8 0.9 repeat_y.1
  12.7 4.2 %all-to-all-start = ((bf16[4,128,768]{2,1,0:T(8,128)(2,1)}), bf16[4,128,768]{2,1,0:T(8,128)(2,1)S(1)}, u32[]{:S(2)}, u32[]{:S(2)}) async-start(bf16[4,128,768]{2,1,0:T(8,128)(2,1)} %repeat_y.1), calls=%async_computation | async-start | bytes 1572864 | tf_op jit(solution)/shard_map/all_to_all | solution.py:58
  16.9 0.0 copy-done.5
  16.9 0.3 gelu.1.refs_0_
  17.2 0.8 collective-permute-start.15
  18.0 0.0 collective-permute-done
  18.0 3.3 %collective-permute-done.1 = bf16[128,768]{1,0:T(8,128)(2,1)S(1)} collective-permute-done((bf16[128,768]{1,0:T(8,128)(2,1)}, bf16[128,768]{1,0:T(8,128)(2,1)S(1)}, u32[]{:S(2)}, u32[]{:S(2)}) %collective-permute-start.1) | collective-permute-done | bytes 196640 | tf_op jit(solution)/shard_map/ppermute | solution.py:31
  21.4 1.4 %collective-permute-done.2 = bf16[128,768]{1,0:T(8,128)(2,1)S(1)} collective-permute-done((bf16[128,768]{1,0:T(8,128)(2,1)}, bf16[128,768]{1,0:T(8,128)(2,1)S(1)}, u32[]{:S(2)}, u32[]{:S(2)}) %collective-permute-start.2) | collective-permute-done | bytes 196640 | tf_op jit(solution)/shard_map/ppermute | solution.py:31
  22.8 2.9 %collective-permute-start.7 = (bf16[1536,768]{1,0:T(8,128)(2,1)}, bf16[1536,768]{1,0:T(8,128)(2,1)}, u32[]{:S(2)}, u32[]{:S(2)}) collective-permute-start(bf16[1536,768]{1,0:T(8,128)(2,1)} %w_own_ref), channel_id=1, source_target_pairs={{16,0},{0,16},{17,1},{1,17},{18,2},{2,18},{19,3},{3,19},{20,4},{4,... | collective-permute-start | bytes 7077896 | tf_op jit(solution)/shard_map/ppermute | solution.py:31
  25.7 0.7 constant_dynamic-update-slice_fusion.2
  26.4 0.7 constant_dynamic-update-slice_fusion.1
  27.1 0.7 constant_dynamic-update-slice_fusion.refs_2_
  27.8 1.3 %collective-permute-start.5 = (bf16[384,768]{1,0:T(8,128)(2,1)}, bf16[384,768]{1,0:T(8,128)(2,1)}, u32[]{:S(2)}, u32[]{:S(2)}) collective-permute-start(bf16[384,768]{1,0:T(8,128)(2,1)} %constant_dynamic-update-slice_fusion.refs_2_), channel_id=1, source_target_pairs={{3,0},{0,1},{1,2},{2,3},{7,4},{4,5},{5,6},{6,7},{11,8},{8,9},{9,10... | collective-permute-start | bytes 1769480 | tf_op jit(solution)/shard_map/ppermute | solution.py:31
  29.1 1.4 %collective-permute-start.3 = (bf16[384,768]{1,0:T(8,128)(2,1)}, bf16[384,768]{1,0:T(8,128)(2,1)}, u32[]{:S(2)}, u32[]{:S(2)}) collective-permute-start(bf16[384,768]{1,0:T(8,128)(2,1)} %constant_dynamic-update-slice_fusion.refs_2_), channel_id=1, source_target_pairs={{1,0},{2,1},{3,2},{0,3},{5,4},{6,5},{7,6},{4,7},{9,8},{10,9},{11,1... | collective-permute-start | bytes 1769480 | tf_op jit(solution)/shard_map/ppermute | solution.py:31
  30.6 1.6 %collective-permute-start.4 = (bf16[384,768]{1,0:T(8,128)(2,1)}, bf16[384,768]{1,0:T(8,128)(2,1)}, u32[]{:S(2)}, u32[]{:S(2)}) collective-permute-start(bf16[384,768]{1,0:T(8,128)(2,1)} %constant_dynamic-update-slice_fusion.refs_2_), channel_id=1, source_target_pairs={{2,0},{3,1},{0,2},{1,3},{6,4},{7,5},{4,6},{5,7},{10,8},{11,9},{8,1... | collective-permute-start | bytes 1769480 | tf_op jit(solution)/shard_map/ppermute | solution.py:31
  32.2 2.2 %collective-permute-done.15.refs_1_ = bf16[128,1536]{1,0:T(8,128)(2,1)S(1)} collective-permute-done((bf16[128,1536]{1,0:T(8,128)(2,1)S(1)}, bf16[128,1536]{1,0:T(8,128)(2,1)S(1)}, u32[]{:S(2)}, u32[]{:S(2)}) %collective-permute-start.15) | collective-permute-done | bytes 393248 | tf_op jit(solution)/shard_map/ppermute | solution.py:31
  34.4 1.7 %repeat_x.1 = bf16[4,256,1536]{2,1,0:T(8,128)(2,1)} custom-call(bf16[128,1536]{1,0:T(8,128)(2,1)S(1)} %gelu.1.refs_0_, bf16[128,1536]{1,0:T(8,128)(2,1)S(1)} %collective-permute-done.15.refs_1_), custom_call_target="tpu_custom_call" | custom-call | tf_op jit(solution)/shard_map/repeat_x/pallas_call | solution.py:49
  36.1 0.0 all-to-all-done
  36.1 0.0 copy-start.2
  36.1 0.9 copy-done.2
  37.0 4.0 %all-to-all-start.1 = ((bf16[4,256,1536]{2,1,0:T(8,128)(2,1)}), bf16[4,256,1536]{2,1,0:T(8,128)(2,1)S(1)}, u32[]{:S(2)}, u32[]{:S(2)}) async-start(bf16[4,256,1536]{2,1,0:T(8,128)(2,1)} %repeat_x.1), calls=%async_computation.1 | async-start | bytes 6291456 | tf_op jit(solution)/shard_map/all_to_all | solution.py:58
  41.0 0.5 slope.1.slope_ref
  41.6 0.9 copy-done.4
  42.5 0.7 dynamic-slice_bitcast_fusion
  43.1 0.1 fusion
  43.2 1.1 %copy-done.3 = bf16[4,128,768]{2,1,0:T(8,128)(2,1)S(1)} copy-done((bf16[4,128,768]{2,1,0:T(8,128)(2,1)S(1)}, bf16[4,128,768]{2,1,0:T(8,128)(2,1)}, u32[]{:S(2)}) %copy-start.3) | copy-done | bytes 786456
  44.4 2.3 %order_tokens_0.1 = (bf16[1024,768]{1,0:T(8,128)(2,1)}, bf16[1024,768]{1,0:T(8,128)(2,1)}) custom-call(s32[16]{0:T(128)S(1)} %get-tuple-element.49.refs_0_, bf16[512,768]{1,0:T(8,128)(2,1)S(1)} %bitcast.6, bf16[384,768]{1,0:T(8,128)(2,1)} %constant_dynamic-update-slice_fusion.refs_2_), custom_call_target="tpu_custom_call" | custom-call | tf_op jit(solution)/shard_map/order_tokens_0/pallas_call | solution.py:124
  46.6 0.0 collective-permute-done.5.refs_1_
  46.6 1.9 %order_tokens_7.1 = (bf16[1024,768]{1,0:T(8,128)(2,1)}, bf16[1024,768]{1,0:T(8,128)(2,1)}) custom-call(s32[16]{0:T(128)S(1)} %get-tuple-element.49.refs_0_, bf16[384,768]{1,0:T(8,128)(2,1)} %collective-permute-done.5.refs_1_, bf16[1024,768]{1,0:T(8,128)(2,1)} %get-tuple-element.30.refs_2_, ...), custom_call_target="tpu_custom_call", output_to_operand_aliasing={{0}: (2, {}), {1}: (3, {})} | custom-call | tf_op jit(solution)/shard_map/order_tokens_7/pallas_call | solution.py:124
  48.6 0.0 collective-permute-done.3.refs_1_
  48.6 9.6 %collective-permute-done.4.refs_2_ = bf16[384,768]{1,0:T(8,128)(2,1)} collective-permute-done((bf16[384,768]{1,0:T(8,128)(2,1)}, bf16[384,768]{1,0:T(8,128)(2,1)}, u32[]{:S(2)}, u32[]{:S(2)}) %collective-permute-start.4) | collective-permute-done | bytes 589856 | tf_op jit(solution)/shard_map/ppermute | solution.py:31
  58.2 2.4 %order_tokens_10.1 = (bf16[1024,768]{1,0:T(8,128)(2,1)}, bf16[1024,768]{1,0:T(8,128)(2,1)}) custom-call(s32[16]{0:T(128)S(1)} %get-tuple-element.49.refs_0_, bf16[384,768]{1,0:T(8,128)(2,1)} %collective-permute-done.3.refs_1_, bf16[384,768]{1,0:T(8,128)(2,1)} %collective-permute-done.4.refs_2_, ...), custom_call_target="tpu_custom_call", output_to_operand_aliasing={{0}: (3, {}), {1}: (4, {})} | custom-call | tf_op jit(solution)/shard_map/order_tokens_10/pallas_call | solution.py:124
  60.5 0.9 collective-permute-start.6
  61.5 3.2 %collective-permute-done.6.other_ref = bf16[1024,768]{1,0:T(8,128)(2,1)S(1)} collective-permute-done((bf16[1024,768]{1,0:T(8,128)(2,1)}, bf16[1024,768]{1,0:T(8,128)(2,1)S(1)}, u32[]{:S(2)}, u32[]{:S(2)}) %collective-permute-start.6) | collective-permute-done | bytes 1572896 | tf_op jit(solution)/shard_map/ppermute | solution.py:31
  64.7 0.0 collective-permute-done.7.w_other_ref
  64.7 8.3 %terms.1 = (bf16[128,1536]{1,0:T(8,128)(2,1)}, bf16[128,1536]{1,0:T(8,128)(2,1)}, bf16[128,1536]{1,0:T(8,128)(2,1)}, bf16[128,1536]{1,0:T(8,128)(2,1)}, bf16[128...) custom-call(bf16[1024,768]{1,0:T(8,128)(2,1)} %get-tuple-element.34.own_ref, ...), custom_call_target="tpu_custom_call" | custom-call | flops 1048576 | bytes 1048576 | tf_op jit(solution)/shard_map/terms/pallas_call | solution.py:152
  73.0 3.6 %collective-permute-start.11 = (bf16[128,1536]{1,0:T(8,128)(2,1)}, bf16[128,1536]{1,0:T(8,128)(2,1)}, u32[]{:S(2)}, u32[]{:S(2)}) collective-permute-start(bf16[128,1536]{1,0:T(8,128)(2,1)} %get-tuple-element.42), channel_id=1, source_target_pairs={{0,32},{32,0},{64,96},{96,64},{128,160},{160,128},{192,224},{224,1... | collective-permute-start | bytes 1179656 | tf_op jit(solution)/shard_map/ppermute | solution.py:66
  76.6 2.5 %collective-permute-start.13 = (bf16[128,1536]{1,0:T(8,128)(2,1)}, bf16[128,1536]{1,0:T(8,128)(2,1)}, u32[]{:S(2)}, u32[]{:S(2)}) collective-permute-start(bf16[128,1536]{1,0:T(8,128)(2,1)} %get-tuple-element.44), channel_id=1, source_target_pairs={{0,192},{32,224},{64,0},{96,32},{128,64},{160,96},{192,128},{224,1... | collective-permute-start | bytes 1179656 | tf_op jit(solution)/shard_map/ppermute | solution.py:66
  79.1 0.0 collective-permute-start.10
  79.1 0.0 collective-permute-start.8
  79.1 2.7 %collective-permute-start.9 = (bf16[128,1536]{1,0:T(8,128)(2,1)}, bf16[128,1536]{1,0:T(8,128)(2,1)}, u32[]{:S(2)}, u32[]{:S(2)}) collective-permute-start(bf16[128,1536]{1,0:T(8,128)(2,1)} %get-tuple-element.39), channel_id=1, source_target_pairs={{0,192},{32,224},{64,0},{96,32},{128,64},{160,96},{192,128},{224,1... | collective-permute-start | bytes 1179656 | tf_op jit(solution)/shard_map/ppermute | solution.py:66
  81.8 0.0 all-to-all-done.1
  81.8 4.3 %collective-permute-done.11.received_ref = bf16[128,1536]{1,0:T(8,128)(2,1)} collective-permute-done((bf16[128,1536]{1,0:T(8,128)(2,1)}, bf16[128,1536]{1,0:T(8,128)(2,1)}, u32[]{:S(2)}, u32[]{:S(2)}) %collective-permute-start.11) | collective-permute-done | bytes 393248 | tf_op jit(solution)/shard_map/ppermute | solution.py:66
  86.1 1.4 %collective-permute-start.16 = (bf16[1024,1536]{1,0:T(8,128)(2,1)S(1)}, bf16[1024,1536]{1,0:T(8,128)(2,1)S(1)}, u32[]{:S(2)}, u32[]{:S(2)}) collective-permute-start(bf16[1024,1536]{1,0:T(8,128)(2,1)S(1)} %bitcast.4), channel_id=1, source_target_pairs={{16,0},{0,16},{17,1},{1,17},{18,2},{2,18},{19,3},{3,19},{20,4},{4,... | collective-permute-start | bytes 9437192 | tf_op jit(solution)/shard_map/ppermute | solution.py:31
  87.5 1.4 %merge.1 = bf16[128,1536]{1,0:T(8,128)(2,1)S(1)} custom-call(f32[128,1536]{1,0:T(8,128)} %get-tuple-element.41.kept_ref, bf16[128,1536]{1,0:T(8,128)(2,1)} %collective-permute-done.11.received_ref), custom_call_target="tpu_custom_call" | custom-call | flops 30000001024 | bytes 1048576 | tf_op jit(solution)/shard_map/merge/pallas_call | solution.py:205
  88.9 0.0 copy-start
  88.9 0.0 collective-permute-done.13
  89.0 2.8 %collective-permute-start.12 = (bf16[128,1536]{1,0:T(8,128)(2,1)S(1)}, bf16[128,1536]{1,0:T(8,128)(2,1)S(1)}, u32[]{:S(2)}, u32[]{:S(2)}) collective-permute-start(bf16[128,1536]{1,0:T(8,128)(2,1)S(1)} %merge.1), channel_id=1, source_target_pairs={{0,128},{32,160},{64,192},{96,224},{128,0},{160,32},{192,64},{224,... | collective-permute-start | bytes 1179656 | tf_op jit(solution)/shard_map/ppermute | solution.py:66
  91.8 0.0 copy-done.7
  91.8 1.1 add_convert_fusion
  92.9 0.0 collective-permute-done.16.act_other_ref
  92.9 1.9 %collective-permute-start.14 = (bf16[128,1536]{1,0:T(8,128)(2,1)S(1)}, bf16[128,1536]{1,0:T(8,128)(2,1)S(1)}, u32[]{:S(2)}, u32[]{:S(2)}) collective-permute-start(bf16[128,1536]{1,0:T(8,128)(2,1)S(1)} %add_convert_fusion), channel_id=1, source_target_pairs={{0,32},{32,0},{64,96},{96,64},{128,160},{160,128},{192,224},{224,1... | collective-permute-start | bytes 1179656 | tf_op jit(solution)/shard_map/ppermute | solution.py:66
  94.7 8.2 %weight_grad.1 = (f32[1536,768]{1,0:T(8,128)}, f32[8,128]{1,0:T(8,128)S(1)}) custom-call(s32[16]{0:T(128)S(1)} %get-tuple-element.48.idx_ref, bf16[1024,1536]{1,0:T(8,128)(2,1)S(1)} %bitcast.5, bf16[1024,1536]{1,0:T(8,128)(2,1)S(1)} %collective-permute-done.16.act_other_ref, bf16[1024,768]{1,0:T(8,128)(2,1)S(1)} %copy-done, bf16[1024,768]{1,0:T(8,128)(2,1)S(1)} %copy-done.1), custom_call_target="tpu_custom_call" | custom-call | flops 4831838208 | bytes 11010048 | tf_op jit(solution)/shard_map/weight_grad/pallas_call | solution.py:185
  102.9 0.0 collective-permute-done.10.refs_2_
  102.9 0.0 collective-permute-done.8.refs_0_
  102.9 0.0 collective-permute-done.9.refs_1_
  102.9 0.5 collective-permute-done.14.refs_4_
  103.5 4.6 %collective-permute-done.12.refs_3_ = bf16[128,1536]{1,0:T(8,128)(2,1)S(1)} collective-permute-done((bf16[128,1536]{1,0:T(8,128)(2,1)S(1)}, bf16[128,1536]{1,0:T(8,128)(2,1)S(1)}, u32[]{:S(2)}, u32[]{:S(2)}) %collective-permute-start.12) | collective-permute-done | bytes 393248 | tf_op jit(solution)/shard_map/ppermute | solution.py:66
  108.0 2.7 %pre_grad.1 = bf16[128,1536]{1,0:T(8,128)(2,1)} custom-call(f32[128,1536]{1,0:T(8,128)} %copy-done.4, f32[128,1536]{1,0:T(8,128)} %get-tuple-element.37.own_ref, bf16[128,1536]{1,0:T(8,128)(2,1)} %collective-permute-done.8.refs_0_, bf16[128,1536]{1,0:T(8,128)(2,1)} %collective-permute-done.9.refs_1_, bf16[128,1536]{1,0:T(8,128)(2,1)S(1)} %collective-permute-done.10.refs_2_, ...), custom_call_target="tpu_custom_call" | custom-call | tf_op jit(solution)/shard_map/pre_grad/pallas_call | solution.py:226
  (7 shorter events, 0.0 us)
Async XLA Ops:
  0.6 16.3 %copy-start.5 = (bf16[128,1536]{1,0:T(8,128)(2,1)S(1)}, bf16[128,1536]{1,0:T(8,128)(2,1)}, u32[]{:S(2)}) copy-start(bf16[128,1536]{1,0:T(8,128)(2,1)} %pre_ref.3) | copy-start | bytes 1179652
  0.6 17.4 %collective-permute-start = (bf16[128,768]{1,0:T(8,128)(2,1)}, bf16[128,768]{1,0:T(8,128)(2,1)S(1)}, u32[]{:S(2)}, u32[]{:S(2)}) collective-permute-start(bf16[128,768]{1,0:T(8,128)(2,1)} %refs_0_.1), channel_id=1, source_target_pairs={{4,0},{8,4},{12,8},{0,12},{5,1},{9,5},{13,9},{1,13},{6,2},{10,6},{... | collective-permute-start | bytes 589832 | tf_op jit(solution)/shard_map/ppermute | solution.py:31
  7.6 13.8 %collective-permute-start.1 = (bf16[128,768]{1,0:T(8,128)(2,1)}, bf16[128,768]{1,0:T(8,128)(2,1)S(1)}, u32[]{:S(2)}, u32[]{:S(2)}) collective-permute-start(bf16[128,768]{1,0:T(8,128)(2,1)} %refs_0_.1), channel_id=1, source_target_pairs={{8,0},{12,4},{0,8},{4,12},{9,1},{13,5},{1,9},{5,13},{10,2},{14,6},... | collective-permute-start | bytes 589832 | tf_op jit(solution)/shard_map/ppermute | solution.py:31
  8.6 14.2 %collective-permute-start.2 = (bf16[128,768]{1,0:T(8,128)(2,1)}, bf16[128,768]{1,0:T(8,128)(2,1)S(1)}, u32[]{:S(2)}, u32[]{:S(2)}) collective-permute-start(bf16[128,768]{1,0:T(8,128)(2,1)} %refs_0_.1), channel_id=1, source_target_pairs={{12,0},{0,4},{4,8},{8,12},{13,1},{1,5},{5,9},{9,13},{14,2},{2,6},{... | collective-permute-start | bytes 589832 | tf_op jit(solution)/shard_map/ppermute | solution.py:31
  10.8 1.0 copy-start.6
  12.7 23.4 %all-to-all-start = ((bf16[4,128,768]{2,1,0:T(8,128)(2,1)}), bf16[4,128,768]{2,1,0:T(8,128)(2,1)S(1)}, u32[]{:S(2)}, u32[]{:S(2)}) async-start(bf16[4,128,768]{2,1,0:T(8,128)(2,1)} %repeat_y.1), calls=%async_computation | async-start | bytes 1572864 | tf_op jit(solution)/shard_map/all_to_all | solution.py:58
  17.2 17.2 %collective-permute-start.15 = (bf16[128,1536]{1,0:T(8,128)(2,1)S(1)}, bf16[128,1536]{1,0:T(8,128)(2,1)S(1)}, u32[]{:S(2)}, u32[]{:S(2)}) collective-permute-start(bf16[128,1536]{1,0:T(8,128)(2,1)S(1)} %gelu.1.refs_0_), channel_id=1, source_target_pairs={{32,0},{0,32},{33,1},{1,33},{34,2},{2,34},{35,3},{3,35},{36,4},{4,... | collective-permute-start | bytes 1179656 | tf_op jit(solution)/shard_map/ppermute | solution.py:31
  22.8 41.9 %collective-permute-start.7 = (bf16[1536,768]{1,0:T(8,128)(2,1)}, bf16[1536,768]{1,0:T(8,128)(2,1)}, u32[]{:S(2)}, u32[]{:S(2)}) collective-permute-start(bf16[1536,768]{1,0:T(8,128)(2,1)} %w_own_ref), channel_id=1, source_target_pairs={{16,0},{0,16},{17,1},{1,17},{18,2},{2,18},{19,3},{3,19},{20,4},{4,... | collective-permute-start | bytes 7077896 | tf_op jit(solution)/shard_map/ppermute | solution.py:31
  27.8 18.8 %collective-permute-start.5 = (bf16[384,768]{1,0:T(8,128)(2,1)}, bf16[384,768]{1,0:T(8,128)(2,1)}, u32[]{:S(2)}, u32[]{:S(2)}) collective-permute-start(bf16[384,768]{1,0:T(8,128)(2,1)} %constant_dynamic-update-slice_fusion.refs_2_), channel_id=1, source_target_pairs={{3,0},{0,1},{1,2},{2,3},{7,4},{4,5},{5,6},{6,7},{11,8},{8,9},{9,10... | collective-permute-start | bytes 1769480 | tf_op jit(solution)/shard_map/ppermute | solution.py:31
  29.1 19.5 %collective-permute-start.3 = (bf16[384,768]{1,0:T(8,128)(2,1)}, bf16[384,768]{1,0:T(8,128)(2,1)}, u32[]{:S(2)}, u32[]{:S(2)}) collective-permute-start(bf16[384,768]{1,0:T(8,128)(2,1)} %constant_dynamic-update-slice_fusion.refs_2_), channel_id=1, source_target_pairs={{1,0},{2,1},{3,2},{0,3},{5,4},{6,5},{7,6},{4,7},{9,8},{10,9},{11,1... | collective-permute-start | bytes 1769480 | tf_op jit(solution)/shard_map/ppermute | solution.py:31
  30.6 27.6 %collective-permute-start.4 = (bf16[384,768]{1,0:T(8,128)(2,1)}, bf16[384,768]{1,0:T(8,128)(2,1)}, u32[]{:S(2)}, u32[]{:S(2)}) collective-permute-start(bf16[384,768]{1,0:T(8,128)(2,1)} %constant_dynamic-update-slice_fusion.refs_2_), channel_id=1, source_target_pairs={{2,0},{3,1},{0,2},{1,3},{6,4},{7,5},{4,6},{5,7},{10,8},{11,9},{8,1... | collective-permute-start | bytes 1769480 | tf_op jit(solution)/shard_map/ppermute | solution.py:31
  36.1 0.9 copy-start.2
  37.0 44.8 %all-to-all-start.1 = ((bf16[4,256,1536]{2,1,0:T(8,128)(2,1)}), bf16[4,256,1536]{2,1,0:T(8,128)(2,1)S(1)}, u32[]{:S(2)}, u32[]{:S(2)}) async-start(bf16[4,256,1536]{2,1,0:T(8,128)(2,1)} %repeat_x.1), calls=%async_computation.1 | async-start | bytes 6291456 | tf_op jit(solution)/shard_map/all_to_all | solution.py:58
  41.5 0.9 copy-start.4
  43.2 1.1 %copy-start.3 = (bf16[4,128,768]{2,1,0:T(8,128)(2,1)S(1)}, bf16[4,128,768]{2,1,0:T(8,128)(2,1)}, u32[]{:S(2)}) copy-start(bf16[4,128,768]{2,1,0:T(8,128)(2,1)} %copy-done.2) | copy-start | bytes 2359300
  60.5 4.2 %collective-permute-start.6 = (bf16[1024,768]{1,0:T(8,128)(2,1)}, bf16[1024,768]{1,0:T(8,128)(2,1)S(1)}, u32[]{:S(2)}, u32[]{:S(2)}) collective-permute-start(bf16[1024,768]{1,0:T(8,128)(2,1)} %get-tuple-element.35.other_ref), channel_id=1, source_target_pairs={{16,0},{0,16},{17,1},{1,17},{18,2},{2,18},{19,3},{3,19},{20,4},{4,... | collective-permute-start | bytes 4718600 | tf_op jit(solution)/shard_map/ppermute | solution.py:31
  73.0 13.1 %collective-permute-start.11 = (bf16[128,1536]{1,0:T(8,128)(2,1)}, bf16[128,1536]{1,0:T(8,128)(2,1)}, u32[]{:S(2)}, u32[]{:S(2)}) collective-permute-start(bf16[128,1536]{1,0:T(8,128)(2,1)} %get-tuple-element.42), channel_id=1, source_target_pairs={{0,32},{32,0},{64,96},{96,64},{128,160},{160,128},{192,224},{224,1... | collective-permute-start | bytes 1179656 | tf_op jit(solution)/shard_map/ppermute | solution.py:66
  76.6 12.3 %collective-permute-start.13 = (bf16[128,1536]{1,0:T(8,128)(2,1)}, bf16[128,1536]{1,0:T(8,128)(2,1)}, u32[]{:S(2)}, u32[]{:S(2)}) collective-permute-start(bf16[128,1536]{1,0:T(8,128)(2,1)} %get-tuple-element.44), channel_id=1, source_target_pairs={{0,192},{32,224},{64,0},{96,32},{128,64},{160,96},{192,128},{224,1... | collective-permute-start | bytes 1179656 | tf_op jit(solution)/shard_map/ppermute | solution.py:66
  79.1 23.8 %collective-permute-start.10 = (bf16[128,1536]{1,0:T(8,128)(2,1)}, bf16[128,1536]{1,0:T(8,128)(2,1)S(1)}, u32[]{:S(2)}, u32[]{:S(2)}) collective-permute-start(bf16[128,1536]{1,0:T(8,128)(2,1)} %get-tuple-element.40), channel_id=1, source_target_pairs={{0,96},{32,64},{64,160},{96,128},{128,224},{160,192},{192,32},{224... | collective-permute-start | bytes 1179656 | tf_op jit(solution)/shard_map/ppermute | solution.py:66
  79.1 23.8 %collective-permute-start.8 = (bf16[128,1536]{1,0:T(8,128)(2,1)}, bf16[128,1536]{1,0:T(8,128)(2,1)}, u32[]{:S(2)}, u32[]{:S(2)}) collective-permute-start(bf16[128,1536]{1,0:T(8,128)(2,1)} %get-tuple-element.38), channel_id=1, source_target_pairs={{0,64},{32,96},{64,128},{96,160},{128,192},{160,224},{192,0},{224,... | collective-permute-start | bytes 1179656 | tf_op jit(solution)/shard_map/ppermute | solution.py:66
  79.1 23.8 %collective-permute-start.9 = (bf16[128,1536]{1,0:T(8,128)(2,1)}, bf16[128,1536]{1,0:T(8,128)(2,1)}, u32[]{:S(2)}, u32[]{:S(2)}) collective-permute-start(bf16[128,1536]{1,0:T(8,128)(2,1)} %get-tuple-element.39), channel_id=1, source_target_pairs={{0,192},{32,224},{64,0},{96,32},{128,64},{160,96},{192,128},{224,1... | collective-permute-start | bytes 1179656 | tf_op jit(solution)/shard_map/ppermute | solution.py:66
  86.1 6.8 %collective-permute-start.16 = (bf16[1024,1536]{1,0:T(8,128)(2,1)S(1)}, bf16[1024,1536]{1,0:T(8,128)(2,1)S(1)}, u32[]{:S(2)}, u32[]{:S(2)}) collective-permute-start(bf16[1024,1536]{1,0:T(8,128)(2,1)S(1)} %bitcast.4), channel_id=1, source_target_pairs={{16,0},{0,16},{17,1},{1,17},{18,2},{2,18},{19,3},{3,19},{20,4},{4,... | collective-permute-start | bytes 9437192 | tf_op jit(solution)/shard_map/ppermute | solution.py:31
  87.5 4.3 %copy-start.7 = (f32[128,1536]{1,0:T(8,128)S(1)}, f32[128,1536]{1,0:T(8,128)}, u32[]{:S(2)}) copy-start(f32[128,1536]{1,0:T(8,128)} %get-tuple-element.43) | copy-start | bytes 2359300
  87.5 7.3 %copy-start.1 = (bf16[1024,768]{1,0:T(8,128)(2,1)S(1)}, bf16[1024,768]{1,0:T(8,128)(2,1)}, u32[]{:S(2)}) copy-start(bf16[1024,768]{1,0:T(8,128)(2,1)} %get-tuple-element.35.other_ref) | copy-start | bytes 4718596
  88.9 5.8 %copy-start = (bf16[1024,768]{1,0:T(8,128)(2,1)S(1)}, bf16[1024,768]{1,0:T(8,128)(2,1)}, u32[]{:S(2)}) copy-start(bf16[1024,768]{1,0:T(8,128)(2,1)} %get-tuple-element.34.own_ref) | copy-start | bytes 4718596
  89.0 19.1 %collective-permute-start.12 = (bf16[128,1536]{1,0:T(8,128)(2,1)S(1)}, bf16[128,1536]{1,0:T(8,128)(2,1)S(1)}, u32[]{:S(2)}, u32[]{:S(2)}) collective-permute-start(bf16[128,1536]{1,0:T(8,128)(2,1)S(1)} %merge.1), channel_id=1, source_target_pairs={{0,128},{32,160},{64,192},{96,224},{128,0},{160,32},{192,64},{224,... | collective-permute-start | bytes 1179656 | tf_op jit(solution)/shard_map/ppermute | solution.py:66
  92.9 10.6 %collective-permute-start.14 = (bf16[128,1536]{1,0:T(8,128)(2,1)S(1)}, bf16[128,1536]{1,0:T(8,128)(2,1)S(1)}, u32[]{:S(2)}, u32[]{:S(2)}) collective-permute-start(bf16[128,1536]{1,0:T(8,128)(2,1)S(1)} %add_convert_fusion), channel_id=1, source_target_pairs={{0,32},{32,0},{64,96},{96,64},{128,160},{160,128},{192,224},{224,1... | collective-permute-start | bytes 1179656 | tf_op jit(solution)/shard_map/ppermute | solution.py:66

commit v4 on v3

--- a/solution.py
+++ b/solution.py
@@ -230,7 +230,7 @@
         out_specs=WHOLE,
         compiler_params=pltpu.CompilerParams(vmem_limit_bytes=8 * MIB),
         name="pre_grad",
-    )(in_hbm(slope), in_hbm(own), *received, after)
+    )(slope, own, *received, after)
 
 
 def token_places():

time: 111 us -> 111 us (level)
    unnamed x18 -> x22, local copies, waits for them, and re-layouts: 5.3 us -> 5.28 us
where the time goes in v4:
time: 111 us; the launch traced here: 110 us
  starting transfers between devices  42.1 us (38%)
  Pallas kernels  30.2 us (27%)
  waiting for transfers between devices  29.3 us (26%)
  local copies, waits for them, and re-layouts  6.76 us (6%)
    ppermute x10, starting transfers between devices, fetch(): return lax.ppermute(value, axis, [((i + ahead) % n, i) for i in range(n)])  20.5 us
    ppermute x10, waiting for transfers between devices, fetch(): return lax.ppermute(value, axis, [((i + ahead) % n, i) for i in range(n)])  19.8 us
    ppermute x7, starting transfers between devices, send_xz(): return lax.ppermute(value, ('x', 'zl'), pairs)  13.4 us
    ppermute x7, waiting for transfers between devices, send_xz(): return lax.ppermute(value, ('x', 'zl'), pairs)  9.5 us
    pallas_call x1, Pallas kernels, terms(): pl.pallas_call(terms_kernel, out_shape=[pltpu.HBM((TB, f), jnp.float32 if...  8.36 us
    all_to_all x2, starting transfers between devices, gather(): return lax.all_to_all(copies, axis, 0, 0).reshape(n * len(values) * TB, f)  8.21 us
    pallas_call x1, Pallas kernels, weight_product(): pl.pallas_call(weight_kernel, out_shape=(jax.ShapeDtypeStruct((f, d), jnp...  8.18 us
    pallas_call x3, Pallas kernels, order(): pl.pallas_call(lambda *refs: order_kernel(first, *refs), out_shape=(out,...  6.58 us
  transfers between devices with their start and end apart: 19, of which 8 were waited for; matrix products, arithmetic and copies ran while one was open for 4% of the time, Pallas kernels for 25%

profile of v4, /device:TPU:1, one launch (start us, length us, event | category | flops | bytes accessed | tf_op | source)
XLA Modules:
  0.0 110.2 jit_solution(1936396453004329020)
XLA Ops:
  0.6 0.0 copy-start.6
  0.6 6.9 %collective-permute-start = (bf16[128,768]{1,0:T(8,128)(2,1)}, bf16[128,768]{1,0:T(8,128)(2,1)S(1)}, u32[]{:S(2)}, u32[]{:S(2)}) collective-permute-start(bf16[128,768]{1,0:T(8,128)(2,1)} %refs_0_.1), channel_id=1, source_target_pairs={{4,0},{8,4},{12,8},{0,12},{5,1},{9,5},{13,9},{1,13},{6,2},{10,6},{... | collective-permute-start | bytes 589832 | tf_op jit(solution)/shard_map/ppermute | solution.py:31
  7.6 1.0 collective-permute-start.1
  8.6 2.3 %collective-permute-start.2 = (bf16[128,768]{1,0:T(8,128)(2,1)}, bf16[128,768]{1,0:T(8,128)(2,1)S(1)}, u32[]{:S(2)}, u32[]{:S(2)}) collective-permute-start(bf16[128,768]{1,0:T(8,128)(2,1)} %refs_0_.1), channel_id=1, source_target_pairs={{12,0},{0,4},{4,8},{8,12},{13,1},{1,5},{5,9},{9,13},{14,2},{2,6},{... | collective-permute-start | bytes 589832 | tf_op jit(solution)/shard_map/ppermute | solution.py:31
  10.8 1.0 copy-done.8
  11.8 0.9 repeat_y.1
  12.7 4.2 %all-to-all-start = ((bf16[4,128,768]{2,1,0:T(8,128)(2,1)}), bf16[4,128,768]{2,1,0:T(8,128)(2,1)S(1)}, u32[]{:S(2)}, u32[]{:S(2)}) async-start(bf16[4,128,768]{2,1,0:T(8,128)(2,1)} %repeat_y.1), calls=%async_computation | async-start | bytes 1572864 | tf_op jit(solution)/shard_map/all_to_all | solution.py:58
  16.9 0.0 copy-done.6
  16.9 0.3 gelu.1.refs_0_
  17.2 0.8 collective-permute-start.15
  18.0 0.0 collective-permute-done
  18.0 3.3 %collective-permute-done.1 = bf16[128,768]{1,0:T(8,128)(2,1)S(1)} collective-permute-done((bf16[128,768]{1,0:T(8,128)(2,1)}, bf16[128,768]{1,0:T(8,128)(2,1)S(1)}, u32[]{:S(2)}, u32[]{:S(2)}) %collective-permute-start.1) | collective-permute-done | bytes 196640 | tf_op jit(solution)/shard_map/ppermute | solution.py:31
  21.4 1.4 %collective-permute-done.2 = bf16[128,768]{1,0:T(8,128)(2,1)S(1)} collective-permute-done((bf16[128,768]{1,0:T(8,128)(2,1)}, bf16[128,768]{1,0:T(8,128)(2,1)S(1)}, u32[]{:S(2)}, u32[]{:S(2)}) %collective-permute-start.2) | collective-permute-done | bytes 196640 | tf_op jit(solution)/shard_map/ppermute | solution.py:31
  22.8 2.9 %collective-permute-start.7 = (bf16[1536,768]{1,0:T(8,128)(2,1)}, bf16[1536,768]{1,0:T(8,128)(2,1)}, u32[]{:S(2)}, u32[]{:S(2)}) collective-permute-start(bf16[1536,768]{1,0:T(8,128)(2,1)} %w_own_ref), channel_id=1, source_target_pairs={{16,0},{0,16},{17,1},{1,17},{18,2},{2,18},{19,3},{3,19},{20,4},{4,... | collective-permute-start | bytes 7077896 | tf_op jit(solution)/shard_map/ppermute | solution.py:31
  25.7 0.7 constant_dynamic-update-slice_fusion.2
  26.4 0.7 constant_dynamic-update-slice_fusion.1
  27.1 0.7 constant_dynamic-update-slice_fusion.refs_2_
  27.8 1.3 %collective-permute-start.5 = (bf16[384,768]{1,0:T(8,128)(2,1)}, bf16[384,768]{1,0:T(8,128)(2,1)}, u32[]{:S(2)}, u32[]{:S(2)}) collective-permute-start(bf16[384,768]{1,0:T(8,128)(2,1)} %constant_dynamic-update-slice_fusion.refs_2_), channel_id=1, source_target_pairs={{3,0},{0,1},{1,2},{2,3},{7,4},{4,5},{5,6},{6,7},{11,8},{8,9},{9,10... | collective-permute-start | bytes 1769480 | tf_op jit(solution)/shard_map/ppermute | solution.py:31
  29.1 1.4 %collective-permute-start.3 = (bf16[384,768]{1,0:T(8,128)(2,1)}, bf16[384,768]{1,0:T(8,128)(2,1)}, u32[]{:S(2)}, u32[]{:S(2)}) collective-permute-start(bf16[384,768]{1,0:T(8,128)(2,1)} %constant_dynamic-update-slice_fusion.refs_2_), channel_id=1, source_target_pairs={{1,0},{2,1},{3,2},{0,3},{5,4},{6,5},{7,6},{4,7},{9,8},{10,9},{11,1... | collective-permute-start | bytes 1769480 | tf_op jit(solution)/shard_map/ppermute | solution.py:31
  30.5 1.6 %collective-permute-start.4 = (bf16[384,768]{1,0:T(8,128)(2,1)}, bf16[384,768]{1,0:T(8,128)(2,1)}, u32[]{:S(2)}, u32[]{:S(2)}) collective-permute-start(bf16[384,768]{1,0:T(8,128)(2,1)} %constant_dynamic-update-slice_fusion.refs_2_), channel_id=1, source_target_pairs={{2,0},{3,1},{0,2},{1,3},{6,4},{7,5},{4,6},{5,7},{10,8},{11,9},{8,1... | collective-permute-start | bytes 1769480 | tf_op jit(solution)/shard_map/ppermute | solution.py:31
  32.2 2.2 %collective-permute-done.15.refs_1_ = bf16[128,1536]{1,0:T(8,128)(2,1)S(1)} collective-permute-done((bf16[128,1536]{1,0:T(8,128)(2,1)S(1)}, bf16[128,1536]{1,0:T(8,128)(2,1)S(1)}, u32[]{:S(2)}, u32[]{:S(2)}) %collective-permute-start.15) | collective-permute-done | bytes 393248 | tf_op jit(solution)/shard_map/ppermute | solution.py:31
  34.4 1.7 %repeat_x.1 = bf16[4,256,1536]{2,1,0:T(8,128)(2,1)} custom-call(bf16[128,1536]{1,0:T(8,128)(2,1)S(1)} %gelu.1.refs_0_, bf16[128,1536]{1,0:T(8,128)(2,1)S(1)} %collective-permute-done.15.refs_1_), custom_call_target="tpu_custom_call" | custom-call | tf_op jit(solution)/shard_map/repeat_x/pallas_call | solution.py:49
  36.1 0.0 all-to-all-done
  36.1 0.0 copy-start.2
  36.1 0.9 copy-done.2
  37.0 4.0 %all-to-all-start.1 = ((bf16[4,256,1536]{2,1,0:T(8,128)(2,1)}), bf16[4,256,1536]{2,1,0:T(8,128)(2,1)S(1)}, u32[]{:S(2)}, u32[]{:S(2)}) async-start(bf16[4,256,1536]{2,1,0:T(8,128)(2,1)} %repeat_x.1), calls=%async_computation.1 | async-start | bytes 6291456 | tf_op jit(solution)/shard_map/all_to_all | solution.py:58
  41.0 0.5 slope.1.slope_ref
  41.6 0.0 copy-start.4
  41.6 0.9 copy-done.4
  42.5 0.7 dynamic-slice_bitcast_fusion
  43.2 0.1 fusion
  43.2 1.1 %copy-done.3 = bf16[4,128,768]{2,1,0:T(8,128)(2,1)S(1)} copy-done((bf16[4,128,768]{2,1,0:T(8,128)(2,1)S(1)}, bf16[4,128,768]{2,1,0:T(8,128)(2,1)}, u32[]{:S(2)}) %copy-start.3) | copy-done | bytes 786456
  44.4 2.3 %order_tokens_0.1 = (bf16[1024,768]{1,0:T(8,128)(2,1)}, bf16[1024,768]{1,0:T(8,128)(2,1)}) custom-call(s32[16]{0:T(128)S(1)} %get-tuple-element.49.refs_0_, bf16[512,768]{1,0:T(8,128)(2,1)S(1)} %bitcast.6, bf16[384,768]{1,0:T(8,128)(2,1)} %constant_dynamic-update-slice_fusion.refs_2_), custom_call_target="tpu_custom_call" | custom-call | tf_op jit(solution)/shard_map/order_tokens_0/pallas_call | solution.py:124
  46.6 0.0 collective-permute-done.5.refs_1_
  46.7 1.9 %order_tokens_7.1 = (bf16[1024,768]{1,0:T(8,128)(2,1)}, bf16[1024,768]{1,0:T(8,128)(2,1)}) custom-call(s32[16]{0:T(128)S(1)} %get-tuple-element.49.refs_0_, bf16[384,768]{1,0:T(8,128)(2,1)} %collective-permute-done.5.refs_1_, bf16[1024,768]{1,0:T(8,128)(2,1)} %get-tuple-element.30.refs_2_, ...), custom_call_target="tpu_custom_call", output_to_operand_aliasing={{0}: (2, {}), {1}: (3, {})} | custom-call | tf_op jit(solution)/shard_map/order_tokens_7/pallas_call | solution.py:124
  48.6 0.0 collective-permute-done.3.refs_1_
  48.6 9.5 %collective-permute-done.4.refs_2_ = bf16[384,768]{1,0:T(8,128)(2,1)} collective-permute-done((bf16[384,768]{1,0:T(8,128)(2,1)}, bf16[384,768]{1,0:T(8,128)(2,1)}, u32[]{:S(2)}, u32[]{:S(2)}) %collective-permute-start.4) | collective-permute-done | bytes 589856 | tf_op jit(solution)/shard_map/ppermute | solution.py:31
  58.1 2.4 %order_tokens_10.1 = (bf16[1024,768]{1,0:T(8,128)(2,1)}, bf16[1024,768]{1,0:T(8,128)(2,1)}) custom-call(s32[16]{0:T(128)S(1)} %get-tuple-element.49.refs_0_, bf16[384,768]{1,0:T(8,128)(2,1)} %collective-permute-done.3.refs_1_, bf16[384,768]{1,0:T(8,128)(2,1)} %collective-permute-done.4.refs_2_, ...), custom_call_target="tpu_custom_call", output_to_operand_aliasing={{0}: (3, {}), {1}: (4, {})} | custom-call | tf_op jit(solution)/shard_map/order_tokens_10/pallas_call | solution.py:124
  60.5 0.9 collective-permute-start.6
  61.4 3.2 %collective-permute-done.6.other_ref = bf16[1024,768]{1,0:T(8,128)(2,1)S(1)} collective-permute-done((bf16[1024,768]{1,0:T(8,128)(2,1)}, bf16[1024,768]{1,0:T(8,128)(2,1)S(1)}, u32[]{:S(2)}, u32[]{:S(2)}) %collective-permute-start.6) | collective-permute-done | bytes 1572896 | tf_op jit(solution)/shard_map/ppermute | solution.py:31
  64.7 0.0 collective-permute-done.7.w_other_ref
  64.7 8.4 %terms.1 = (bf16[128,1536]{1,0:T(8,128)(2,1)}, bf16[128,1536]{1,0:T(8,128)(2,1)}, bf16[128,1536]{1,0:T(8,128)(2,1)}, bf16[128,1536]{1,0:T(8,128)(2,1)}, bf16[128...) custom-call(bf16[1024,768]{1,0:T(8,128)(2,1)} %get-tuple-element.34.own_ref, ...), custom_call_target="tpu_custom_call" | custom-call | flops 1048576 | bytes 1048576 | tf_op jit(solution)/shard_map/terms/pallas_call | solution.py:152
  73.0 3.6 %collective-permute-start.11 = (bf16[128,1536]{1,0:T(8,128)(2,1)}, bf16[128,1536]{1,0:T(8,128)(2,1)}, u32[]{:S(2)}, u32[]{:S(2)}) collective-permute-start(bf16[128,1536]{1,0:T(8,128)(2,1)} %get-tuple-element.42), channel_id=1, source_target_pairs={{0,32},{32,0},{64,96},{96,64},{128,160},{160,128},{192,224},{224,1... | collective-permute-start | bytes 1179656 | tf_op jit(solution)/shard_map/ppermute | solution.py:66
  76.6 2.4 %collective-permute-start.13 = (bf16[128,1536]{1,0:T(8,128)(2,1)}, bf16[128,1536]{1,0:T(8,128)(2,1)}, u32[]{:S(2)}, u32[]{:S(2)}) collective-permute-start(bf16[128,1536]{1,0:T(8,128)(2,1)} %get-tuple-element.44), channel_id=1, source_target_pairs={{0,192},{32,224},{64,0},{96,32},{128,64},{160,96},{192,128},{224,1... | collective-permute-start | bytes 1179656 | tf_op jit(solution)/shard_map/ppermute | solution.py:66
  79.1 0.0 collective-permute-start.10
  79.1 0.0 collective-permute-start.8
  79.1 2.7 %collective-permute-start.9 = (bf16[128,1536]{1,0:T(8,128)(2,1)}, bf16[128,1536]{1,0:T(8,128)(2,1)}, u32[]{:S(2)}, u32[]{:S(2)}) collective-permute-start(bf16[128,1536]{1,0:T(8,128)(2,1)} %get-tuple-element.39), channel_id=1, source_target_pairs={{0,192},{32,224},{64,0},{96,32},{128,64},{160,96},{192,128},{224,1... | collective-permute-start | bytes 1179656 | tf_op jit(solution)/shard_map/ppermute | solution.py:66
  81.8 0.0 all-to-all-done.1
  81.8 4.4 %collective-permute-done.11.received_ref = bf16[128,1536]{1,0:T(8,128)(2,1)} collective-permute-done((bf16[128,1536]{1,0:T(8,128)(2,1)}, bf16[128,1536]{1,0:T(8,128)(2,1)}, u32[]{:S(2)}, u32[]{:S(2)}) %collective-permute-start.11) | collective-permute-done | bytes 393248 | tf_op jit(solution)/shard_map/ppermute | solution.py:66
  86.1 1.4 %collective-permute-start.16 = (bf16[1024,1536]{1,0:T(8,128)(2,1)S(1)}, bf16[1024,1536]{1,0:T(8,128)(2,1)S(1)}, u32[]{:S(2)}, u32[]{:S(2)}) collective-permute-start(bf16[1024,1536]{1,0:T(8,128)(2,1)S(1)} %bitcast.4), channel_id=1, source_target_pairs={{16,0},{0,16},{17,1},{1,17},{18,2},{2,18},{19,3},{3,19},{20,4},{4,... | collective-permute-start | bytes 9437192 | tf_op jit(solution)/shard_map/ppermute | solution.py:31
  87.5 1.4 %merge.1 = bf16[128,1536]{1,0:T(8,128)(2,1)S(1)} custom-call(f32[128,1536]{1,0:T(8,128)} %get-tuple-element.41.kept_ref, bf16[128,1536]{1,0:T(8,128)(2,1)} %collective-permute-done.11.received_ref), custom_call_target="tpu_custom_call" | custom-call | flops 30000001024 | bytes 1048576 | tf_op jit(solution)/shard_map/merge/pallas_call | solution.py:205
  89.0 0.0 collective-permute-done.13
  89.0 2.8 %collective-permute-start.12 = (bf16[128,1536]{1,0:T(8,128)(2,1)S(1)}, bf16[128,1536]{1,0:T(8,128)(2,1)S(1)}, u32[]{:S(2)}, u32[]{:S(2)}) collective-permute-start(bf16[128,1536]{1,0:T(8,128)(2,1)S(1)} %merge.1), channel_id=1, source_target_pairs={{0,128},{32,160},{64,192},{96,224},{128,0},{160,32},{192,64},{224,... | collective-permute-start | bytes 1179656 | tf_op jit(solution)/shard_map/ppermute | solution.py:66
  91.8 1.1 add_convert_fusion
  92.8 0.0 collective-permute-done.16.act_other_ref
  92.9 1.9 %collective-permute-start.14 = (bf16[128,1536]{1,0:T(8,128)(2,1)S(1)}, bf16[128,1536]{1,0:T(8,128)(2,1)S(1)}, u32[]{:S(2)}, u32[]{:S(2)}) collective-permute-start(bf16[128,1536]{1,0:T(8,128)(2,1)S(1)} %add_convert_fusion), channel_id=1, source_target_pairs={{0,32},{32,0},{64,96},{96,64},{128,160},{160,128},{192,224},{224,1... | collective-permute-start | bytes 1179656 | tf_op jit(solution)/shard_map/ppermute | solution.py:66
  94.7 8.2 %weight_grad.1 = (f32[1536,768]{1,0:T(8,128)}, f32[8,128]{1,0:T(8,128)S(1)}) custom-call(s32[16]{0:T(128)S(1)} %get-tuple-element.48.idx_ref, bf16[1024,1536]{1,0:T(8,128)(2,1)S(1)} %bitcast.5, bf16[1024,1536]{1,0:T(8,128)(2,1)S(1)} %collective-permute-done.16.act_other_ref, bf16[1024,768]{1,0:T(8,128)(2,1)S(1)} %copy-done, bf16[1024,768]{1,0:T(8,128)(2,1)S(1)} %copy-done.1), custom_call_target="tpu_custom_call" | custom-call | flops 4831838208 | bytes 11010048 | tf_op jit(solution)/shard_map/weight_grad/pallas_call | solution.py:185
  102.9 0.0 collective-permute-done.10.refs_2_
  102.9 0.0 collective-permute-done.8.refs_0_
  102.9 0.0 collective-permute-done.9.refs_1_
  102.9 0.5 collective-permute-done.14.refs_4_
  103.5 4.6 %collective-permute-done.12.refs_3_ = bf16[128,1536]{1,0:T(8,128)(2,1)S(1)} collective-permute-done((bf16[128,1536]{1,0:T(8,128)(2,1)S(1)}, bf16[128,1536]{1,0:T(8,128)(2,1)S(1)}, u32[]{:S(2)}, u32[]{:S(2)}) %collective-permute-start.12) | collective-permute-done | bytes 393248 | tf_op jit(solution)/shard_map/ppermute | solution.py:66
  108.0 0.0 copy-done.7
  108.0 2.2 %pre_grad.1 = bf16[128,1536]{1,0:T(8,128)(2,1)} custom-call(f32[128,1536]{1,0:T(8,128)S(1)} %copy-done.5, f32[128,1536]{1,0:T(8,128)S(1)} %copy-done.7, bf16[128,1536]{1,0:T(8,128)(2,1)} %collective-permute-done.8.refs_0_, bf16[128,1536]{1,0:T(8,128)(2,1)} %collective-permute-done.9.refs_1_, bf16[128,1536]{1,0:T(8,128)(2,1)S(1)} %collective-permute-done.10.refs_2_, ...), custom_call_target="tpu_custom_call" | custom-call | tf_op jit(solution)/shard_map/pre_grad/pallas_call | solution.py:226
  (11 shorter events, 0.0 us)
Async XLA Ops:
  0.6 16.3 %copy-start.6 = (bf16[128,1536]{1,0:T(8,128)(2,1)S(1)}, bf16[128,1536]{1,0:T(8,128)(2,1)}, u32[]{:S(2)}) copy-start(bf16[128,1536]{1,0:T(8,128)(2,1)} %pre_ref.3) | copy-start | bytes 1179652
  0.6 17.4 %collective-permute-start = (bf16[128,768]{1,0:T(8,128)(2,1)}, bf16[128,768]{1,0:T(8,128)(2,1)S(1)}, u32[]{:S(2)}, u32[]{:S(2)}) collective-permute-start(bf16[128,768]{1,0:T(8,128)(2,1)} %refs_0_.1), channel_id=1, source_target_pairs={{4,0},{8,4},{12,8},{0,12},{5,1},{9,5},{13,9},{1,13},{6,2},{10,6},{... | collective-permute-start | bytes 589832 | tf_op jit(solution)/shard_map/ppermute | solution.py:31
  7.6 13.8 %collective-permute-start.1 = (bf16[128,768]{1,0:T(8,128)(2,1)}, bf16[128,768]{1,0:T(8,128)(2,1)S(1)}, u32[]{:S(2)}, u32[]{:S(2)}) collective-permute-start(bf16[128,768]{1,0:T(8,128)(2,1)} %refs_0_.1), channel_id=1, source_target_pairs={{8,0},{12,4},{0,8},{4,12},{9,1},{13,5},{1,9},{5,13},{10,2},{14,6},... | collective-permute-start | bytes 589832 | tf_op jit(solution)/shard_map/ppermute | solution.py:31
  8.6 14.2 %collective-permute-start.2 = (bf16[128,768]{1,0:T(8,128)(2,1)}, bf16[128,768]{1,0:T(8,128)(2,1)S(1)}, u32[]{:S(2)}, u32[]{:S(2)}) collective-permute-start(bf16[128,768]{1,0:T(8,128)(2,1)} %refs_0_.1), channel_id=1, source_target_pairs={{12,0},{0,4},{4,8},{8,12},{13,1},{1,5},{5,9},{9,13},{14,2},{2,6},{... | collective-permute-start | bytes 589832 | tf_op jit(solution)/shard_map/ppermute | solution.py:31
  10.8 1.0 copy-start.8
  12.7 23.4 %all-to-all-start = ((bf16[4,128,768]{2,1,0:T(8,128)(2,1)}), bf16[4,128,768]{2,1,0:T(8,128)(2,1)S(1)}, u32[]{:S(2)}, u32[]{:S(2)}) async-start(bf16[4,128,768]{2,1,0:T(8,128)(2,1)} %repeat_y.1), calls=%async_computation | async-start | bytes 1572864 | tf_op jit(solution)/shard_map/all_to_all | solution.py:58
  17.2 17.2 %collective-permute-start.15 = (bf16[128,1536]{1,0:T(8,128)(2,1)S(1)}, bf16[128,1536]{1,0:T(8,128)(2,1)S(1)}, u32[]{:S(2)}, u32[]{:S(2)}) collective-permute-start(bf16[128,1536]{1,0:T(8,128)(2,1)S(1)} %gelu.1.refs_0_), channel_id=1, source_target_pairs={{32,0},{0,32},{33,1},{1,33},{34,2},{2,34},{35,3},{3,35},{36,4},{4,... | collective-permute-start | bytes 1179656 | tf_op jit(solution)/shard_map/ppermute | solution.py:31
  22.8 41.9 %collective-permute-start.7 = (bf16[1536,768]{1,0:T(8,128)(2,1)}, bf16[1536,768]{1,0:T(8,128)(2,1)}, u32[]{:S(2)}, u32[]{:S(2)}) collective-permute-start(bf16[1536,768]{1,0:T(8,128)(2,1)} %w_own_ref), channel_id=1, source_target_pairs={{16,0},{0,16},{17,1},{1,17},{18,2},{2,18},{19,3},{3,19},{20,4},{4,... | collective-permute-start | bytes 7077896 | tf_op jit(solution)/shard_map/ppermute | solution.py:31
  27.8 18.9 %collective-permute-start.5 = (bf16[384,768]{1,0:T(8,128)(2,1)}, bf16[384,768]{1,0:T(8,128)(2,1)}, u32[]{:S(2)}, u32[]{:S(2)}) collective-permute-start(bf16[384,768]{1,0:T(8,128)(2,1)} %constant_dynamic-update-slice_fusion.refs_2_), channel_id=1, source_target_pairs={{3,0},{0,1},{1,2},{2,3},{7,4},{4,5},{5,6},{6,7},{11,8},{8,9},{9,10... | collective-permute-start | bytes 1769480 | tf_op jit(solution)/shard_map/ppermute | solution.py:31
  29.1 19.5 %collective-permute-start.3 = (bf16[384,768]{1,0:T(8,128)(2,1)}, bf16[384,768]{1,0:T(8,128)(2,1)}, u32[]{:S(2)}, u32[]{:S(2)}) collective-permute-start(bf16[384,768]{1,0:T(8,128)(2,1)} %constant_dynamic-update-slice_fusion.refs_2_), channel_id=1, source_target_pairs={{1,0},{2,1},{3,2},{0,3},{5,4},{6,5},{7,6},{4,7},{9,8},{10,9},{11,1... | collective-permute-start | bytes 1769480 | tf_op jit(solution)/shard_map/ppermute | solution.py:31
  30.5 27.6 %collective-permute-start.4 = (bf16[384,768]{1,0:T(8,128)(2,1)}, bf16[384,768]{1,0:T(8,128)(2,1)}, u32[]{:S(2)}, u32[]{:S(2)}) collective-permute-start(bf16[384,768]{1,0:T(8,128)(2,1)} %constant_dynamic-update-slice_fusion.refs_2_), channel_id=1, source_target_pairs={{2,0},{3,1},{0,2},{1,3},{6,4},{7,5},{4,6},{5,7},{10,8},{11,9},{8,1... | collective-permute-start | bytes 1769480 | tf_op jit(solution)/shard_map/ppermute | solution.py:31
  36.1 0.9 copy-start.2
  37.0 44.7 %all-to-all-start.1 = ((bf16[4,256,1536]{2,1,0:T(8,128)(2,1)}), bf16[4,256,1536]{2,1,0:T(8,128)(2,1)S(1)}, u32[]{:S(2)}, u32[]{:S(2)}) async-start(bf16[4,256,1536]{2,1,0:T(8,128)(2,1)} %repeat_x.1), calls=%async_computation.1 | async-start | bytes 6291456 | tf_op jit(solution)/shard_map/all_to_all | solution.py:58
  41.6 0.9 copy-start.4
  43.2 1.1 %copy-start.3 = (bf16[4,128,768]{2,1,0:T(8,128)(2,1)S(1)}, bf16[4,128,768]{2,1,0:T(8,128)(2,1)}, u32[]{:S(2)}) copy-start(bf16[4,128,768]{2,1,0:T(8,128)(2,1)} %copy-done.2) | copy-start | bytes 2359300
  60.5 4.1 %collective-permute-start.6 = (bf16[1024,768]{1,0:T(8,128)(2,1)}, bf16[1024,768]{1,0:T(8,128)(2,1)S(1)}, u32[]{:S(2)}, u32[]{:S(2)}) collective-permute-start(bf16[1024,768]{1,0:T(8,128)(2,1)} %get-tuple-element.35.other_ref), channel_id=1, source_target_pairs={{16,0},{0,16},{17,1},{1,17},{18,2},{2,18},{19,3},{3,19},{20,4},{4,... | collective-permute-start | bytes 4718600 | tf_op jit(solution)/shard_map/ppermute | solution.py:31
  73.0 13.1 %collective-permute-start.11 = (bf16[128,1536]{1,0:T(8,128)(2,1)}, bf16[128,1536]{1,0:T(8,128)(2,1)}, u32[]{:S(2)}, u32[]{:S(2)}) collective-permute-start(bf16[128,1536]{1,0:T(8,128)(2,1)} %get-tuple-element.42), channel_id=1, source_target_pairs={{0,32},{32,0},{64,96},{96,64},{128,160},{160,128},{192,224},{224,1... | collective-permute-start | bytes 1179656 | tf_op jit(solution)/shard_map/ppermute | solution.py:66
  76.6 12.3 %collective-permute-start.13 = (bf16[128,1536]{1,0:T(8,128)(2,1)}, bf16[128,1536]{1,0:T(8,128)(2,1)}, u32[]{:S(2)}, u32[]{:S(2)}) collective-permute-start(bf16[128,1536]{1,0:T(8,128)(2,1)} %get-tuple-element.44), channel_id=1, source_target_pairs={{0,192},{32,224},{64,0},{96,32},{128,64},{160,96},{192,128},{224,1... | collective-permute-start | bytes 1179656 | tf_op jit(solution)/shard_map/ppermute | solution.py:66
  79.1 23.8 %collective-permute-start.10 = (bf16[128,1536]{1,0:T(8,128)(2,1)}, bf16[128,1536]{1,0:T(8,128)(2,1)S(1)}, u32[]{:S(2)}, u32[]{:S(2)}) collective-permute-start(bf16[128,1536]{1,0:T(8,128)(2,1)} %get-tuple-element.40), channel_id=1, source_target_pairs={{0,96},{32,64},{64,160},{96,128},{128,224},{160,192},{192,32},{224... | collective-permute-start | bytes 1179656 | tf_op jit(solution)/shard_map/ppermute | solution.py:66
  79.1 23.8 %collective-permute-start.8 = (bf16[128,1536]{1,0:T(8,128)(2,1)}, bf16[128,1536]{1,0:T(8,128)(2,1)}, u32[]{:S(2)}, u32[]{:S(2)}) collective-permute-start(bf16[128,1536]{1,0:T(8,128)(2,1)} %get-tuple-element.38), channel_id=1, source_target_pairs={{0,64},{32,96},{64,128},{96,160},{128,192},{160,224},{192,0},{224,... | collective-permute-start | bytes 1179656 | tf_op jit(solution)/shard_map/ppermute | solution.py:66
  79.1 23.8 %collective-permute-start.9 = (bf16[128,1536]{1,0:T(8,128)(2,1)}, bf16[128,1536]{1,0:T(8,128)(2,1)}, u32[]{:S(2)}, u32[]{:S(2)}) collective-permute-start(bf16[128,1536]{1,0:T(8,128)(2,1)} %get-tuple-element.39), channel_id=1, source_target_pairs={{0,192},{32,224},{64,0},{96,32},{128,64},{160,96},{192,128},{224,1... | collective-permute-start | bytes 1179656 | tf_op jit(solution)/shard_map/ppermute | solution.py:66
  86.1 6.7 %collective-permute-start.16 = (bf16[1024,1536]{1,0:T(8,128)(2,1)S(1)}, bf16[1024,1536]{1,0:T(8,128)(2,1)S(1)}, u32[]{:S(2)}, u32[]{:S(2)}) collective-permute-start(bf16[1024,1536]{1,0:T(8,128)(2,1)S(1)} %bitcast.4), channel_id=1, source_target_pairs={{16,0},{0,16},{17,1},{1,17},{18,2},{2,18},{19,3},{3,19},{20,4},{4,... | collective-permute-start | bytes 9437192 | tf_op jit(solution)/shard_map/ppermute | solution.py:31
  87.5 4.3 %copy-start.9 = (f32[128,1536]{1,0:T(8,128)S(1)}, f32[128,1536]{1,0:T(8,128)}, u32[]{:S(2)}) copy-start(f32[128,1536]{1,0:T(8,128)} %get-tuple-element.43) | copy-start | bytes 2359300
  87.5 7.2 %copy-start.1 = (bf16[1024,768]{1,0:T(8,128)(2,1)S(1)}, bf16[1024,768]{1,0:T(8,128)(2,1)}, u32[]{:S(2)}) copy-start(bf16[1024,768]{1,0:T(8,128)(2,1)} %get-tuple-element.35.other_ref) | copy-start | bytes 4718596
  89.0 5.8 %copy-start = (bf16[1024,768]{1,0:T(8,128)(2,1)S(1)}, bf16[1024,768]{1,0:T(8,128)(2,1)}, u32[]{:S(2)}) copy-start(bf16[1024,768]{1,0:T(8,128)(2,1)} %get-tuple-element.34.own_ref) | copy-start | bytes 4718596
  89.0 19.0 %collective-permute-start.12 = (bf16[128,1536]{1,0:T(8,128)(2,1)S(1)}, bf16[128,1536]{1,0:T(8,128)(2,1)S(1)}, u32[]{:S(2)}, u32[]{:S(2)}) collective-permute-start(bf16[128,1536]{1,0:T(8,128)(2,1)S(1)} %merge.1), channel_id=1, source_target_pairs={{0,128},{32,160},{64,192},{96,224},{128,0},{160,32},{192,64},{224,... | collective-permute-start | bytes 1179656 | tf_op jit(solution)/shard_map/ppermute | solution.py:66
  92.9 10.6 %collective-permute-start.14 = (bf16[128,1536]{1,0:T(8,128)(2,1)S(1)}, bf16[128,1536]{1,0:T(8,128)(2,1)S(1)}, u32[]{:S(2)}, u32[]{:S(2)}) collective-permute-start(bf16[128,1536]{1,0:T(8,128)(2,1)S(1)} %add_convert_fusion), channel_id=1, source_target_pairs={{0,32},{32,0},{64,96},{96,64},{128,160},{160,128},{192,224},{224,1... | collective-permute-start | bytes 1179656 | tf_op jit(solution)/shard_map/ppermute | solution.py:66
  94.7 13.3 %copy-start.5 = (f32[128,1536]{1,0:T(8,128)S(1)}, f32[128,1536]{1,0:T(8,128)}, u32[]{:S(2)}) copy-start(f32[128,1536]{1,0:T(8,128)} %copy-done.4) | copy-start | bytes 2359300
  94.7 13.3 %copy-start.7 = (f32[128,1536]{1,0:T(8,128)S(1)}, f32[128,1536]{1,0:T(8,128)}, u32[]{:S(2)}) copy-start(f32[128,1536]{1,0:T(8,128)} %get-tuple-element.37.own_ref) | copy-start | bytes 2359300
